TPU v7x, 128 devices: a whole 4x4x4 slice. The times are simulated.
128 devices in a mesh: pipe: 4 (over y), dp: 32 (over z, x, core).
Axes of the slice: x: 4, y: 4, z: 4, core: 2. Of those that a mesh axis runs over, the one named last changes fastest.
Arguments:
- cotangent: bfloat16 [2, 128, 4096], P(None, None, 'dp'), may hold values from -4 to 4
- stashed_inputs: bfloat16 [4, 2, 128, 4096], P('pipe', None, None, 'dp'), may hold values from -4 to 4
- weights: bfloat16 [4, 4096, 4096], P('pipe', 'dp'), may hold values from -0.09375 to 0.09375
- momentum: bfloat16 [4, 4096, 4096], P('pipe', 'dp'), may hold values from -560 to 560
Outputs:
- input_grads: bfloat16 [4, 2, 128, 4096], P('pipe', None, None, 'dp')
- new_momentum: bfloat16 [4, 4096, 4096], P('pipe', 'dp')
- orth_update: bfloat16 [4, 4096, 4096], P('pipe', 'dp')
All inputs are finite; a program needn't handle non-finite values.
Results may differ from a plain program's by a relative error of at most 0.008.
Values may be sent and summed in bfloat16 or wider, within the bound.
A program may use at most 192 MiB of HBM per device.

v0:
```python
import math

import jax
import jax.numpy as jnp
from jax import lax
from jax.sharding import PartitionSpec as P

quintic_a = 3.4445
quintic_b = -4.775
quintic_c = 2.0315


def from_behind(value, axis, steps):
    count = lax.axis_size(axis)
    leading, last = (max(0, -steps), min(count, count - steps))
    return lax.ppermute(value, axis, [(source, source + steps) for source in range(leading, last)])


def contract_last(left_part, right_part):
    return lax.dot_general(
        left_part, right_part, (((1,), (1,)), ((), ())), preferred_element_type=jnp.float32
    )


def per_device(cotangent, stashed_inputs, weights, momentum):
    layers = lax.axis_size("pipe")
    section = lax.axis_index("pipe")
    micro_count = cotangent.shape[0]
    tok_rows = cotangent.shape[1]
    width_loc = cotangent.shape[2]
    weight_rows = weights[0]
    width_full = weight_rows.shape[1]
    activations = stashed_inputs[0].astype(jnp.float32)
    sigmoid_val = jax.nn.sigmoid(activations)
    slopes = sigmoid_val * (1.0 + activations * (1.0 - sigmoid_val))
    gated_acts = (activations * sigmoid_val).astype(jnp.bfloat16)
    incoming = jnp.zeros((tok_rows, width_loc), jnp.bfloat16)
    out_grads = jnp.zeros((micro_count, tok_rows, width_loc), jnp.bfloat16)
    weight_grad = jnp.zeros((width_loc, width_full), jnp.float32)
    steps_all = micro_count + layers - 1
    for step_index in range(steps_all):
        micro_index = step_index - (layers - 1 - section)
        is_valid = (micro_index >= 0) & (micro_index < micro_count)
        slot_index = jnp.clip(micro_index, 0, micro_count - 1)
        own_grad = lax.dynamic_index_in_dim(cotangent, slot_index, 0, keepdims=False)
        upstream = jnp.where(section == layers - 1, own_grad, incoming)
        full_grad = lax.all_gather(upstream, "dp", axis=1, tiled=True)
        back_proj = contract_last(full_grad, weight_rows)
        slope_now = lax.dynamic_index_in_dim(slopes, slot_index, 0, keepdims=False)
        dinput = (upstream.astype(jnp.float32) + slope_now * back_proj).astype(jnp.bfloat16)
        out_grads = jnp.where(
            is_valid, lax.dynamic_update_index_in_dim(out_grads, dinput, slot_index, 0), out_grads
        )
        gated_now = lax.dynamic_index_in_dim(gated_acts, slot_index, 0, keepdims=False)
        weight_term = lax.dot_general(
            gated_now, full_grad, (((0,), (0,)), ((), ())), preferred_element_type=jnp.float32
        )
        weight_grad = weight_grad + jnp.where(is_valid, weight_term, 0.0)
        if step_index + 1 < steps_all:
            incoming = from_behind(dinput, "pipe", -1)
    entries = float(width_full) * float(width_full)
    fresh_moment = (0.95 * momentum[0].astype(jnp.float32) + weight_grad).astype(jnp.bfloat16)
    fresh32 = fresh_moment.astype(jnp.float32)
    sum_squares = lax.psum(jnp.sum(fresh32 * fresh32), "dp")
    scaling = 0.4 / jnp.sqrt(width_full * (sum_squares / entries + 1e-06))
    scaled_rows = (fresh32 * scaling).astype(jnp.bfloat16)
    whole_matrix = lax.all_gather(scaled_rows, "dp", axis=0, tiled=True)
    gram_rows = contract_last(scaled_rows, whole_matrix).astype(jnp.bfloat16)
    cubic_rows = jnp.dot(gram_rows, whole_matrix, preferred_element_type=jnp.float32).astype(
        jnp.bfloat16
    )
    back_rows = contract_last(cubic_rows, whole_matrix).astype(jnp.bfloat16)
    quintic_rows = jnp.dot(back_rows, whole_matrix, preferred_element_type=jnp.float32)
    mixed = (
        quintic_a * scaled_rows.astype(jnp.float32)
        + quintic_b * cubic_rows.astype(jnp.float32)
        + quintic_c * quintic_rows
    )
    update_rows = (math.sqrt(width_full) * mixed).astype(jnp.bfloat16)
    return (out_grads[None], fresh_moment[None], update_rows[None])


def solution(mesh):
    in_specs = (
        P(None, None, "dp"),
        P("pipe", None, None, "dp"),
        P("pipe", "dp", None),
        P("pipe", "dp", None),
    )
    out_specs = (P("pipe", None, None, "dp"), P("pipe", "dp", None), P("pipe", "dp", None))
    return jax.shard_map(
        per_device, mesh=mesh, in_specs=in_specs, out_specs=out_specs, check_vma=False
    )
```

profile of v0, /device:TPU:1, one launch (start us, length us, event | category | flops | bytes accessed | tf_op | source)
XLA Modules:
  0.0 517.5 jit_solution(9246325424143566442)
XLA Ops:
  7.2 0.0 all-gather.18.cloned.1.call-start
  7.2 1.5 dynamic-slice_select_fusion
  8.7 0.0 all-gather.18.cloned.1.call-update
  8.7 0.0 all-gather.8.cloned.1.call-start
  8.8 0.9 fusion.26
  9.7 47.8 %all-gather.18.cloned.1.call-done = bf16[1,128,4096]{2,1,0:T(8,128)(2,1)} async-done(((bf16[1,128,128]{2,1,0:T(8,128)(2,1)}), bf16[1,128,4096]{2,1,0:T(8,128)(2,1)}) %all-gather.18.cloned.1.call-update) | async-done | bytes 1048592 | tf_op jit(solution)/shard_map/all_gather | solution.py:47
  57.6 1.7 bitcast_dynamic-update-slice_fusion
  59.2 1.3 collective-permute-start
  60.6 3.4 collective-permute-done
  63.9 0.6 bitcast_select_fusion.6
  64.5 0.0 all-gather.8.cloned.1.call-update
  64.6 0.0 all-gather.10.cloned.1.call-start
  64.6 43.6 %all-gather.8.cloned.1.call-done = bf16[128,4096]{1,0:T(8,128)(2,1)} async-done(((bf16[128,128]{1,0:T(8,128)(2,1)}), bf16[128,4096]{1,0:T(8,128)(2,1)}) %all-gather.8.cloned.1.call-update) | async-done | bytes 1048592 | tf_op jit(solution)/shard_map/all_gather | solution.py:47
  108.2 1.7 fusion.38
  109.9 1.3 collective-permute-start.1
  111.2 3.4 collective-permute-done.1
  114.6 0.6 bitcast_select_fusion.4
  115.2 0.0 all-gather.10.cloned.1.call-update
  115.2 0.0 all-gather.12.cloned.1.call-start
  115.3 43.6 %all-gather.10.cloned.1.call-done = bf16[128,4096]{1,0:T(8,128)(2,1)} async-done(((bf16[128,128]{1,0:T(8,128)(2,1)}), bf16[128,4096]{1,0:T(8,128)(2,1)}) %all-gather.10.cloned.1.call-update) | async-done | bytes 1048592 | tf_op jit(solution)/shard_map/all_gather | solution.py:47
  158.9 1.7 fusion.37
  160.6 1.3 collective-permute-start.2
  161.9 3.4 collective-permute-done.2
  165.3 0.6 bitcast_select_fusion.2
  165.9 0.0 all-gather.12.cloned.1.call-update
  165.9 0.0 all-gather.14.cloned.1.call-start
  166.0 43.6 %all-gather.12.cloned.1.call-done = bf16[128,4096]{1,0:T(8,128)(2,1)} async-done(((bf16[128,128]{1,0:T(8,128)(2,1)}), bf16[128,4096]{1,0:T(8,128)(2,1)}) %all-gather.12.cloned.1.call-update) | async-done | bytes 1048592 | tf_op jit(solution)/shard_map/all_gather | solution.py:47
  209.6 1.7 fusion.36
  211.3 1.3 collective-permute-start.3
  212.6 3.4 collective-permute-done.3
  215.9 0.6 bitcast_select_fusion
  216.6 0.0 all-gather.14.cloned.1.call-update
  216.6 0.0 all-gather.16.cloned.1.call-start
  216.6 1.7 convolution_select_fusion.4
  218.3 3.1 convolution_select_fusion.2
  221.5 1.8 convolution_select_fusion.1
  223.2 37.0 %all-gather.14.cloned.1.call-done = bf16[128,4096]{1,0:T(8,128)(2,1)} async-done(((bf16[128,128]{1,0:T(8,128)(2,1)}), bf16[128,4096]{1,0:T(8,128)(2,1)}) %all-gather.14.cloned.1.call-update) | async-done | bytes 1048592 | tf_op jit(solution)/shard_map/all_gather | solution.py:47
  260.3 1.8 convolution_select_fusion
  262.1 0.1 copy-done.2
  262.2 0.3 copy-done.3
  262.4 4.6 fusion.10
  267.0 63.1 %psum.7 = f32[]{:T(128)} all-reduce(f32[]{:T(128)} %get-tuple-element.13), channel_id=1, replica_groups=mesh['pipe'=4,'dp'=32] {'dp'}, use_global_device_ids=true, to_apply=%region_1.2 | all-reduce | flops 1 | bytes 8 | tf_op jit(solution)/shard_map/psum | solution.py:64
  330.8 2.4 fusion.11
  333.2 0.0 all-gather.16.cloned.1.call-update
  333.3 0.5 fusion.30
  333.7 112.8 %all-gather.16.cloned.1.call-done = bf16[4096,4096]{1,0:T(8,128)(2,1)} async-done(((bf16[128,4096]{1,0:T(8,128)(2,1)}), bf16[4096,4096]{1,0:T(8,128)(2,1)}) %all-gather.16.cloned.1.call-update) | async-done | bytes 33554448 | tf_op jit(solution)/shard_map/all_gather | solution.py:67
  446.5 31.3 %convolution_convert_fusion.1 = bf16[128,4096]{1,0:T(8,128)(2,1)S(1)} fusion(bf16[4096,4096]{1,0:T(8,128)(2,1)} %all-gather.16.cloned.1.call-done, bf16[128,4096]{1,0:T(8,128)(2,1)S(1)} %copy-done.1), kind=kOutput, calls=%fused_computation.15 | convolution fusion | flops 8590983168 | bytes 35651584 | tf_op jit(solution)/shard_map/dot_general | solution.py:69
  477.9 32.8 %fusion.9 = bf16[1,128,4096]{2,1,0:T(8,128)(2,1)} fusion(bf16[4096,4096]{1,0:T(8,128)(2,1)} %all-gather.16.cloned.1.call-done, bf16[128,4096]{1,0:T(8,128)(2,1)S(1)} %convolution_convert_fusion.1, bf16[128,4096]{1,0:T(8,128)(2,1)S(1)} %copy-done.1), kind=kOutput, calls=%fused_computation.18 | convolution fusion | flops 8595177472 | bytes 36700160 | tf_op jit(solution)/shard_map/dot_general | solution.py:73
  (18 shorter events, 0.1 us)
Async XLA Ops:
  7.2 50.4 %copy-start = (bf16[1,128,4096]{2,1,0:T(8,128)(2,1)S(1)}, bf16[1,128,4096]{2,1,0:T(8,128)(2,1)}, u32[]{:S(2)}) copy-start(bf16[1,128,4096]{2,1,0:T(8,128)(2,1)} %param.6) | copy-start | bytes 3145732
  7.2 56.7 %copy-start.6 = (bf16[2,128,128]{2,1,0:T(8,128)(2,1)S(1)}, bf16[2,128,128]{2,1,0:T(8,128)(2,1)}, u32[]{:S(2)}) copy-start(bf16[2,128,128]{2,1,0:T(8,128)(2,1)} %param.4) | copy-start | bytes 196612
  7.2 50.3 %all-gather.18.cloned.1.call-start = ((), (), s32[]{:S(2)}) async-start(), calls=%async_computation.5 | async-start | bytes 1081344 | tf_op jit(solution)/shard_map/all_gather | solution.py:47
  8.7 99.5 %all-gather.8.cloned.1.call-start = ((), (), s32[]{:S(2)}) async-start(), calls=%async_computation | async-start | bytes 1081344 | tf_op jit(solution)/shard_map/all_gather | solution.py:47
  59.2 4.7 collective-permute-start
  64.6 94.4 %all-gather.10.cloned.1.call-start = ((), (), s32[]{:S(2)}) async-start(), calls=%async_computation.1 | async-start | bytes 1081344 | tf_op jit(solution)/shard_map/all_gather | solution.py:47
  109.9 4.7 collective-permute-start.1
  115.2 94.4 %all-gather.12.cloned.1.call-start = ((), (), s32[]{:S(2)}) async-start(), calls=%async_computation.2 | async-start | bytes 1081344 | tf_op jit(solution)/shard_map/all_gather | solution.py:47
  160.6 4.7 collective-permute-start.2
  165.9 94.4 %all-gather.14.cloned.1.call-start = ((), (), s32[]{:S(2)}) async-start(), calls=%async_computation.3 | async-start | bytes 1081344 | tf_op jit(solution)/shard_map/all_gather | solution.py:47
  211.3 4.7 collective-permute-start.3
  216.6 229.9 %all-gather.16.cloned.1.call-start = ((), (), s32[]{:S(2)}) async-start(), calls=%async_computation.4 | async-start | bytes 34603008 | tf_op jit(solution)/shard_map/all_gather | solution.py:67
  218.3 3.1 copy-start.5
  260.3 1.9 copy-start.2
  260.3 2.2 copy-start.3
  267.0 66.2 %copy-start.4 = (bf16[128,4096]{1,0:T(8,128)(2,1)S(1)}, bf16[128,4096]{1,0:T(8,128)(2,1)}, u32[]{:S(2)}) copy-start(bf16[128,4096]{1,0:T(8,128)(2,1)} %all-gather.14.cloned.1.call-done) | copy-start | bytes 3145732
  267.0 66.2 %copy-start.7 = (bf16[128,128]{1,0:T(8,128)(2,1)S(1)}, bf16[128,128]{1,0:T(8,128)(2,1)}, u32[]{:S(2)}) copy-start(bf16[128,128]{1,0:T(8,128)(2,1)} %bitcast_select_fusion) | copy-start | bytes 98308
  333.2 113.3 %copy-start.1 = (bf16[128,4096]{1,0:T(8,128)(2,1)S(1)}, bf16[128,4096]{1,0:T(8,128)(2,1)}, u32[]{:S(2)}) copy-start(bf16[128,4096]{1,0:T(8,128)(2,1)} %fusion.11) | copy-start | bytes 3145732
  333.7 144.2 %copy-start.8 = (bf16[1,2,128,128]{3,2,1,0:T(8,128)(2,1)}, bf16[1,2,128,128]{3,2,1,0:T(8,128)(2,1)S(1)}, u32[]{:S(2)}) copy-start(bf16[1,2,128,128]{3,2,1,0:T(8,128)(2,1)S(1)} %fusion.30) | copy-start | bytes 196612
Sparse Core Ops, SparseCore 0:
  10.8 46.7 all-gather.17
  64.7 43.5 all-gather.7
  115.4 43.5 all-gather.9
  166.0 43.5 all-gather.11
  216.7 43.5 all-gather.13
  333.4 113.1 all-gather.15
where the time goes:
time: 518 us
  waiting for transfers between devices  342 us (66%)
  matrix products  84.3 us (16%)
  blocking collectives  63.1 us (12%)
  between operations  15 us (3%)
  other arithmetic  7.25 us (1%)
  starting transfers between devices  5.41 us (1%)
    all_gather x5, waiting for transfers between devices, per_device(): full_grad = lax.all_gather(upstream, 'dp', axis=1, tiled=True)  216 us
    all_gather x1, waiting for transfers between devices, per_device(): whole_matrix = lax.all_gather(scaled_rows, 'dp', axis=0, tiled=True)  113 us
    psum x1, blocking collectives, per_device(): sum_squares = lax.psum(jnp.sum(fresh32 * fresh32), 'dp')  63.1 us
    dot_general x1, matrix products, per_device(): jnp.dot(back_rows, whole_matrix, preferred_element_type=jnp.float32)  32.8 us
    dot_general x1, matrix products, per_device(): jnp.dot(gram_rows, whole_matrix, preferred_element_type=jnp.float32)  31.3 us
    ppermute x4, waiting for transfers between devices, from_behind(): lax.ppermute(value, axis, [(source, source + steps) for source in range(l...  13.4 us
    dot_general x5, matrix products, per_device(): lax.dot_general(gated_now, full_grad, (((0,), (0,)), ((), ())), preferred...  13 us
  transfers between devices with their start and end apart: 10, of which 10 were waited for; matrix products, arithmetic and copies ran while one was open for 2% of the time, Pallas kernels for 0%

commit v1 on v0

v1 whole, which is shorter than its diff:
```python
import functools
import math

import jax
import jax.numpy as jnp
from jax import lax
from jax.experimental import pallas as pl
from jax.experimental.pallas import tpu as pltpu
from jax.sharding import PartitionSpec as P

quintic_a = 3.4445
quintic_b = -4.775
quintic_c = 2.0315

MESH = pl.DeviceIdType.MESH
BF = jnp.bfloat16
F32 = jnp.float32
RING = 4
CHIPS = 16
LANE = 128
WIDTH = 4096
HALF = 2048
TOKENS = 256
ROWS = 256
NT = (((1,), (1,)), ((), ()))
NN = (((1,), (0,)), ((), ()))


def place():
    spot = lax.axis_index("dp")
    return lax.axis_index("pipe"), spot // 8, (spot // 2) % RING, spot % 2


def at(y, z, x, core):
    return (y, ((z % RING) * RING + x % RING) * 2 + core)


def chip_of(z, x):
    return (z % RING) * RING + x % RING


def multiple(value, of):
    return pl.multiple_of(value, of)


def offset_of(index):
    return index + (index // 2) * (5 - 2 * index)


class Gather:
    def __init__(self, slot, send, recv):
        self.slot, self.send, self.recv = slot, send, recv
        self.y, self.z, self.x, self.core = place()

    def block(self, part, first, second):
        if part == 0:
            return chip_of(self.z + second, self.x + first)
        return chip_of(self.z + first, self.x + second)

    def target(self, part, axis, steps):
        along_x = (axis == 0) == (part == 0)
        if along_x:
            return at(self.y, self.z, self.x + steps, self.core)
        return at(self.y, self.z + steps, self.x, self.core)

    def copy(self, part, first, second, half, axis, steps, number):
        block = self.block(part, first, second)
        ref = self.slot(block, part, half)
        return pltpu.make_async_remote_copy(
            src_ref=ref,
            dst_ref=ref,
            send_sem=self.send.at[number],
            recv_sem=self.recv.at[block, part, half],
            device_id=self.target(part, axis, steps),
            device_id_type=MESH,
        )

    def put(self, part, first, second, half, axis, steps, number):
        self.copy(part, first, second, half, axis, steps, number).start()

    def wait(self, part, first, second, half):
        self.copy(part, first, second, half, 0, 1, 0).wait_recv()

    def sent(self, number, part=0, half=0):
        self.copy(part, 0, 0, half, 0, 1, number).wait_send()


def step_kernel(
    cot, xs, w, m, dout, nout, oout,
    mbuf, nbuf, wbuf, ubuf, gbuf, xin, slope, dbuf, bsend, brecv, bown, apart, aother, fpart, fother,
    eacc, ebf, qacc, obuf, own_sum, other_sum, own_all, other_all,
    lsem, sib_send, sib_recv, msend, mrecv, gsend, grecv, usend, urecv,
    asend, arecv, fsend, frecv, osem, orecv, nsem, nrecv,
):
    y, z, x, core = place()
    me = chip_of(z, x)
    sibling = at(y, z, x, 1 - core)

    def remote(src, dst, send_sem, recv_sem, device=sibling):
        return pltpu.make_async_remote_copy(
            src_ref=src, dst_ref=dst, send_sem=send_sem, recv_sem=recv_sem,
            device_id=device, device_id_type=MESH,
        )

    partners = [at(y, z, x + 1, core), at(y, z, x + 2, core), at(y, z, x + 3, core),
                at(y, z + 1, x, core), at(y, z + 2, x, core), at(y, z + 3, x, core),
                sibling, at((y + 1) % RING, z, x, core), at((y + 3) % RING, z, x, core)]
    load_x = pltpu.make_async_copy(xs.at[0], xin, lsem.at[0])
    load_x.start()
    barrier = pltpu.get_barrier_semaphore()
    for partner in partners:
        pl.semaphore_signal(barrier, 1, device_id=partner, device_id_type=MESH)

    def row(core_at, height=LANE):
        return pl.ds(multiple(me * ROWS + core_at * LANE, LANE), height)

    def own_columns(k, core_at):
        return pl.ds(multiple((2 * k + core_at) * LANE, LANE), LANE)

    def load_own(k, carry):
        lanes = pl.ds(multiple(k * LANE, LANE), LANE)
        pltpu.make_async_copy(m.at[0, :, own_columns(k, core)], mbuf.at[row(core), lanes], lsem.at[1]).start()
        pltpu.make_async_copy(w.at[0, :, own_columns(k, core)], wbuf.at[core, :, lanes], lsem.at[2]).start()
        return carry

    lax.fori_loop(0, CHIPS, load_own, 0)
    pl.semaphore_wait(barrier, len(partners))

    def give_sibling(k, carry):
        lanes = pl.ds(multiple(k * LANE, LANE), LANE)
        remote(m.at[0, :, own_columns(k, 1 - core)], mbuf.at[row(core), lanes],
               sib_send.at[0], sib_recv.at[0]).start()
        remote(w.at[0, :, own_columns(k, 1 - core)], wbuf.at[core, :, lanes],
               sib_send.at[1], sib_recv.at[1]).start()
        return carry

    lax.fori_loop(0, CHIPS, give_sibling, 0)

    load_x.wait()
    values = xin[...].reshape(TOKENS, LANE).astype(F32)
    sigmoid_val = jax.nn.sigmoid(values)
    slope[...] = sigmoid_val * (1.0 + values * (1.0 - sigmoid_val))
    gated = (values * sigmoid_val).astype(BF).astype(F32)
    gbuf[core, pl.ds(multiple(me * LANE, LANE), LANE), :] = jnp.transpose(gated).astype(BF)

    def m_slot(block, part, half):
        return mbuf.at[pl.ds(multiple(block * ROWS + part * LANE + half * 64, 64), 64), :]

    def g_slot(block, part, half):
        return gbuf.at[core, pl.ds(multiple(block * LANE + part * 64 + half * 32, 32), 32), :]

    def u_slot(block, part, half):
        return ubuf.at[pl.ds(part * LANE, LANE), pl.ds(multiple(block * LANE, LANE), LANE)]

    bulk = [Gather(m_slot, msend, mrecv), Gather(g_slot, gsend, grecv)]
    few = Gather(u_slot, usend, urecv)

    def own_u():
        return ubuf.at[:, pl.ds(multiple(me * LANE, LANE), LANE)]

    def from_above():
        return remote(dbuf, own_u(), sib_send.at[3], sib_recv.at[3], at((y + 3) % RING, z, x, core))

    def chain():
        @pl.when(y == RING - 1)
        def _():
            for micro in range(2):
                pltpu.make_async_copy(
                    cot.at[micro],
                    ubuf.at[pl.ds(micro * LANE, LANE), pl.ds(multiple(me * LANE, LANE), LANE)],
                    lsem.at[3]).start()
            pltpu.make_async_copy(own_u(), own_u(), lsem.at[3]).wait()

        @pl.when(y < RING - 1)
        def _():
            from_above().wait_recv()

        number = 0
        for axis in (0, 1):
            for part in (0, 1):
                for steps in (1, 3, 2):
                    few.put(part, 0, 0, 0, axis, steps, number)
                    number += 1
        for first in (1, 3, 2):
            for part in (0, 1):
                few.wait(part, first, 0, 0)
                for steps in (1, 3, 2):
                    few.put(part, first, 0, 0, 1, steps, number)
                    number += 1
        for first in (0, 1, 3, 2):
            for part in (0, 1):
                for second in (1, 3, 2):
                    few.wait(part, first, second, 0)
        pltpu.make_async_copy(wbuf.at[core], wbuf.at[core], lsem.at[2]).wait()
        remote(wbuf.at[core], wbuf.at[core], sib_send.at[1], sib_recv.at[1]).wait_recv()
        full = ubuf[...]
        bsend[...] = lax.dot_general(full, wbuf[1 - core], NT, preferred_element_type=F32)
        give = remote(bsend, brecv, sib_send.at[2], sib_recv.at[2])
        give.start()
        bown[...] = lax.dot_general(full, wbuf[core], NT, preferred_element_type=F32)
        give.wait()
        back = bown[...] + brecv[...]
        upstream = ubuf[:, pl.ds(multiple(me * LANE, LANE), LANE)].astype(F32)
        dbuf[...] = (upstream + slope[...] * back).astype(BF)

        @pl.when(y > 0)
        def _():
            from_above().start()

        for micro in range(2):
            pltpu.make_async_copy(
                dbuf.at[pl.ds(micro * LANE, LANE), :], dout.at[0, micro], lsem.at[4]).start()

        @pl.when(y > 0)
        def _():
            from_above().wait_send()

    pltpu.make_async_copy(mbuf.at[row(core)], mbuf.at[row(core)], lsem.at[1]).wait()
    remote(mbuf.at[row(core)], mbuf.at[row(core)], sib_send.at[0], sib_recv.at[0]).wait_recv()

    def begin():
        for part in (0, 1):
            for half in (0, 1):
                for steps in (1, 3):
                    for one in bulk:
                        one.put(part, 0, 0, half, 0, steps, 48 + part * 4 + half * 2 + steps // 2)

    def phase(index):
        first = offset_of(index)

        @pl.when((index > 0) & (index < 4))
        def _():
            for part in (0, 1):
                for one in bulk:
                    one.wait(part, first, 0, 0)
                    one.wait(part, first, 0, 1)

        @pl.when(index == 1)
        def _():
            for part in (0, 1):
                for one in bulk:
                    one.put(part, 1, 0, 1, 0, 3, 56 + part * 2)

        @pl.when(index == 2)
        def _():
            for part in (0, 1):
                for one in bulk:
                    one.put(part, 3, 0, 0, 0, 1, 57 + part * 2)

        @pl.when(index < 4)
        def _():
            for part in (0, 1):
                for half in (0, 1):
                    for steps in (1, 3):
                        for one in bulk:
                            one.put(part, first, 0, half, 1, steps,
                                    index * 12 + part * 6 + half * 2 + steps // 2)

        @pl.when(index > 0)
        def _():
            before = offset_of(index - 1)
            for part in (0, 1):
                for one in bulk:
                    one.wait(part, before, 3, 0)
                    one.put(part, before, 3, 0, 1, 1, (index - 1) * 12 + part * 6 + 4)
                    one.wait(part, before, 1, 1)
                    one.put(part, before, 1, 1, 1, 3, (index - 1) * 12 + part * 6 + 5)

    begin()

    def phases(index, carry):
        @pl.when(index == RING - 1 - y)
        def _():
            chain()

        phase(index)
        return carry

    lax.fori_loop(0, RING + 1, phases, 0)

    def arrivals(index, carry):
        first = offset_of(index)
        for part in (0, 1):
            for one in bulk:
                one.wait(part, first, 3, 1)
                one.wait(part, first, 1, 0)
                one.wait(part, first, 2, 0)
                one.wait(part, first, 2, 1)
        return carry

    lax.fori_loop(0, RING, arrivals, 0)
    relay = remote(gbuf.at[core], gbuf.at[core], sib_send.at[4], sib_recv.at[4])
    relay.start()
    relay.wait_send()
    remote(gbuf.at[1 - core], gbuf.at[1 - core], sib_send.at[4], sib_recv.at[4]).wait_recv()

    def rows_of(block, height=ROWS):
        return pl.ds(multiple(block * ROWS, ROWS), height)

    def build(block, total):
        for part in (0, 1):
            where = pl.ds(multiple(block * ROWS + part * LANE, LANE), LANE)
            grad = lax.dot_general(
                gbuf[part, pl.ds(multiple(block * LANE, LANE), LANE), :], ubuf[...], NN,
                preferred_element_type=F32)
            fresh = (0.95 * mbuf[where, :].astype(F32) + grad).astype(BF)
            nbuf[where, :] = fresh
            wide = fresh.astype(F32)
            square = wide * wide
            total = total + jnp.sum(square.reshape(16, 8, 16, LANE), axis=(0, 2))
        return total

    zero = jnp.zeros((8, LANE), F32)
    total = build(me, zero)
    own_sum[...] = total
    swap = remote(own_sum, other_sum, sib_send.at[5], sib_recv.at[5])
    swap.start()
    def give_rows(buf, base, out, sem, recv):
        def body(k, carry):
            lanes = pl.ds(multiple(k * LANE, LANE), LANE)
            pltpu.make_async_copy(
                buf.at[pl.ds(multiple(base + core * LANE, LANE), LANE), lanes],
                out.at[0, :, own_columns(k, core)], sem.at[0]).start()
            remote(buf.at[pl.ds(multiple(base + (1 - core) * LANE, LANE), LANE), lanes],
                   out.at[0, :, own_columns(k, core)], sem.at[1], recv).start()
            return carry
        lax.fori_loop(0, CHIPS, body, 0)

    def wait_rows(buf, out, sem, recv):
        pltpu.make_async_copy(buf.at[pl.ds(0, LANE), :], buf.at[pl.ds(0, LANE), :], sem.at[0]).wait()
        both = remote(buf.at[pl.ds(0, LANE), :], buf.at[pl.ds(0, LANE), :], sem.at[1], recv)
        both.wait_send()
        both.wait_recv()

    give_rows(nbuf, me * ROWS, nout, nsem, nrecv)
    swap.wait()
    chip_norm = jnp.sqrt(jnp.maximum(jnp.sum(own_sum[...] + other_sum[...]), 1e-30))
    inverse = 1.0 / chip_norm

    def a_copy(block):
        return remote(apart.at[block], aother.at[block], asend.at[block], arecv.at[block])

    def f_copy(block):
        return remote(fpart.at[block], fother.at[block], fsend.at[block], frecv.at[block])

    def gram(block):
        part = lax.dot_general(nbuf[rows_of(me), :], nbuf[rows_of(block), :], NT,
                               preferred_element_type=F32)
        apart[block] = (part * inverse).astype(BF)
        a_copy(block).start()

    def cubic(block):
        a_copy(block).wait_recv()
        whole = (apart[block].astype(F32) + aother[block].astype(F32)).astype(BF)
        eacc[...] += lax.dot_general(whole, nbuf[rows_of(block), :], NN, preferred_element_type=F32)

    def turn(index):
        return (me + index) % CHIPS

    eacc[...] = jnp.zeros_like(eacc)
    gram(me)

    def stream(index, total):
        block = turn(index)
        total = build(block, total)
        gram(block)
        cubic(turn(index - 1))
        return total

    total = lax.fori_loop(1, CHIPS, stream, total)
    own_all[...] = total
    swap_all = remote(own_all, other_all, sib_send.at[6], sib_recv.at[6])
    swap_all.start()
    cubic(turn(CHIPS - 1))
    swap_all.wait()
    sum_squares = jnp.sum(own_all[...] + other_all[...])
    scaling = 0.4 / jnp.sqrt(float(WIDTH) * (sum_squares / float(WIDTH * WIDTH) + 1e-06))
    ebf[...] = (((eacc[...] * scaling) * scaling) * (scaling * chip_norm)).astype(BF)

    def back_part(block):
        part = lax.dot_general(ebf[...], nbuf[rows_of(block), :], NT, preferred_element_type=F32)
        fpart[block] = (part * scaling).astype(BF)
        f_copy(block).start()

    def quintic(block):
        f_copy(block).wait_recv()
        whole = (fpart[block].astype(F32) + fother[block].astype(F32)).astype(BF)
        qacc[...] += lax.dot_general(whole, nbuf[rows_of(block), :], NN, preferred_element_type=F32)

    qacc[...] = jnp.zeros_like(qacc)
    back_part(turn(0))
    back_part(turn(1))

    def tail(index, carry):
        back_part(turn(index))
        quintic(turn(index - 2))
        return carry

    lax.fori_loop(2, CHIPS, tail, 0)
    quintic(turn(CHIPS - 2))
    quintic(turn(CHIPS - 1))
    scaled = (nbuf[rows_of(me), :].astype(F32) * scaling).astype(BF).astype(F32)
    mixed = (quintic_a * scaled + quintic_b * ebf[...].astype(F32)
             + quintic_c * (qacc[...] * scaling))
    obuf[...] = (math.sqrt(WIDTH) * mixed).astype(BF)
    give_rows(obuf, 0, oout, osem, orecv)

    pltpu.make_async_copy(dbuf, dbuf, lsem.at[4]).wait()
    remote(mbuf.at[row(core)], mbuf.at[row(core)], sib_send.at[0], sib_recv.at[0]).wait_send()
    remote(wbuf.at[core], wbuf.at[core], sib_send.at[1], sib_recv.at[1]).wait_send()

    def drain_bulk(number, carry):
        for one in bulk:
            one.sent(number)
        return carry

    lax.fori_loop(0, 60, drain_bulk, 0)

    def drain_few(number, carry):
        few.sent(number)
        return carry

    lax.fori_loop(0, 30, drain_few, 0)

    def drain_pairs(block, carry):
        a_copy(block).wait_send()
        f_copy(block).wait_send()
        return carry

    lax.fori_loop(0, CHIPS, drain_pairs, 0)
    wait_rows(nbuf, nout, nsem, nrecv)
    wait_rows(obuf, oout, osem, orecv)


def per_device(cotangent, stashed_inputs, weights, momentum):
    anywhere = pl.BlockSpec(memory_space=pl.ANY)
    sem = pltpu.SemaphoreType.DMA
    scratch = [
        pltpu.VMEM((WIDTH, HALF), BF),
        pltpu.VMEM((WIDTH, HALF), BF),
        pltpu.VMEM((2, LANE, HALF), BF),
        pltpu.VMEM((TOKENS, HALF), BF),
        pltpu.VMEM((2, CHIPS * LANE, TOKENS), BF),
        pltpu.VMEM((2, LANE, LANE), BF),
        pltpu.VMEM((TOKENS, LANE), F32),
        pltpu.VMEM((TOKENS, LANE), BF),
        pltpu.VMEM((TOKENS, LANE), F32),
        pltpu.VMEM((TOKENS, LANE), F32),
        pltpu.VMEM((TOKENS, LANE), F32),
        pltpu.VMEM((CHIPS, ROWS, ROWS), BF),
        pltpu.VMEM((CHIPS, ROWS, ROWS), BF),
        pltpu.VMEM((CHIPS, ROWS, ROWS), BF),
        pltpu.VMEM((CHIPS, ROWS, ROWS), BF),
        pltpu.VMEM((ROWS, HALF), F32),
        pltpu.VMEM((ROWS, HALF), BF),
        pltpu.VMEM((ROWS, HALF), F32),
        pltpu.VMEM((ROWS, HALF), BF),
        pltpu.VMEM((8, LANE), F32),
        pltpu.VMEM((8, LANE), F32),
        pltpu.VMEM((8, LANE), F32),
        pltpu.VMEM((8, LANE), F32),
        sem((5,)),
        sem((7,)),
        sem((7,)),
        sem((60,)),
        sem((CHIPS, 2, 2)),
        sem((60,)),
        sem((CHIPS, 2, 2)),
        sem((30,)),
        sem((CHIPS, 2, 1)),
        sem((CHIPS,)),
        sem((CHIPS,)),
        sem((CHIPS,)),
        sem((CHIPS,)),
        sem((2,)),
        sem,
        sem((2,)),
        sem,
    ]
    return pl.pallas_call(
        step_kernel,
        out_shape=(
            jax.ShapeDtypeStruct(stashed_inputs.shape, BF),
            jax.ShapeDtypeStruct(momentum.shape, BF),
            jax.ShapeDtypeStruct(momentum.shape, BF),
        ),
        in_specs=[anywhere] * 4,
        out_specs=(anywhere, anywhere, anywhere),
        scratch_shapes=scratch,
        compiler_params=pltpu.CompilerParams(
            collective_id=0, has_side_effects=True, vmem_limit_bytes=60 * 1024 * 1024),
        cost_estimate=pl.CostEstimate(
            flops=22 * 10**9, bytes_accessed=6 * 2**20, transcendentals=32768),
    )(cotangent, stashed_inputs, weights, momentum)


def solution(mesh):
    in_specs = (
        P(None, None, "dp"),
        P("pipe", None, None, "dp"),
        P("pipe", "dp", None),
        P("pipe", "dp", None),
    )
    out_specs = (P("pipe", None, None, "dp"), P("pipe", "dp", None), P("pipe", "dp", None))
    return jax.shard_map(
        per_device, mesh=mesh, in_specs=in_specs, out_specs=out_specs, check_vma=False
    )
```

time: 518 us -> 198 us (0.38)
  the two profiles are of different devices: /device:TPU:1 before, /device:TPU:9 now
where the time goes in v1:
time: 198 us
  Pallas kernels  193 us (97%)
  local copies, waits for them, and re-layouts  4.82 us (2%)
    pallas_call x1, Pallas kernels, per_device(): pl.pallas_call(step_kernel, out_shape=(jax.ShapeDtypeStruct(stashed_input...  193 us
    unnamed x5, local copies, waits for them, and re-layouts  4.82 us

profile of v1, /device:TPU:9, one launch (start us, length us, event | category | flops | bytes accessed | tf_op | source)
XLA Modules:
  0.0 198.1 jit_solution(9994527665018213518)
XLA Ops:
  0.6 192.6 %shard_map.67 = (bf16[1,2,128,128]{3,2,1,0:T(8,128)(2,1)}, bf16[1,128,4096]{2,1,0:T(8,128)(2,1)}, bf16[1,128,4096]{2,1,0:T(8,128)(2,1)}) custom-call(bf16[2,128,128]{2,1,0:T(8,128)(2,1)} %cot.1, bf16[1,2,128,128]{3,2,1,0:T(8,128)(2,1)} %xs.1, bf16[1,128,4096]{2,1,0:T(8,128)(2,1)} %w.1, bf16[1,128,4096]{2,1,0:T(8,128)(2,1)} %m.1), custom_call_target="tpu_custom_call" | custom-call | flops 22000001024 | bytes 6291456 | tf_op jit(solution)/shard_map/pallas_call | solution.py:480
  193.3 1.5 copy.10
  194.8 0.0 copy-start
  194.8 2.4 %copy.11 = bf16[1,128,4096]{2,1,0:T(8,128)(2,1)} copy(bf16[1,128,4096]{2,1,0:T(8,128)(2,1)} %get-tuple-element.7) | data formatting | bytes 2097152
  197.1 0.0 copy-done
  197.1 1.0 copy.12
Async XLA Ops:
  194.8 2.4 %copy-start = (bf16[1,128,4096]{2,1,0:T(8,128)(2,1)S(1)}, bf16[1,128,4096]{2,1,0:T(8,128)(2,1)}, u32[]{:S(2)}) copy-start(bf16[1,128,4096]{2,1,0:T(8,128)(2,1)} %get-tuple-element.8) | copy-start | bytes 3145732

commit v2 on v0

v2 whole, which is shorter than its diff:
```python
import functools
import math

import jax
import jax.numpy as jnp
from jax import lax
from jax.experimental import pallas as pl
from jax.experimental.pallas import tpu as pltpu
from jax.sharding import PartitionSpec as P

quintic_a = 3.4445
quintic_b = -4.775
quintic_c = 2.0315

MESH = pl.DeviceIdType.MESH
BF = jnp.bfloat16
F32 = jnp.float32
RING = 4
CHIPS = 16
LANE = 128
WIDTH = 4096
HALF = 2048
TOKENS = 256
ROWS = 256
OFFSETS = (0, 1, 3, 2)
NT = (((1,), (1,)), ((), ()))
NN = (((1,), (0,)), ((), ()))


def place():
    spot = lax.axis_index("dp")
    return lax.axis_index("pipe"), spot // 8, (spot // 2) % RING, spot % 2


def at(y, z, x, core):
    return (y, ((z % RING) * RING + x % RING) * 2 + core)


def chip_of(z, x):
    return (z % RING) * RING + x % RING


def multiple(value, of):
    return pl.multiple_of(value, of)


def ring(value, steps):
    return (value + steps) % RING


class Plane:
    def __init__(self):
        self.y, self.z, self.x, self.core = place()
        self.sibling = at(self.y, self.z, self.x, 1 - self.core)

    def own(self, part):
        return (self.x, self.z) if part == 0 else (self.z, self.x)

    def spot(self, part, first, second):
        own_first, own_second = self.own(part)
        return ring(own_first, first), ring(own_second, second)

    def target(self, part, axis, steps):
        along_x = (axis == 0) == (part == 0)
        if along_x:
            return at(self.y, self.z, self.x + steps, self.core)
        return at(self.y, self.z + steps, self.x, self.core)

    def remote(self, src, dst, send_sem, recv_sem, device=None):
        return pltpu.make_async_remote_copy(
            src_ref=src, dst_ref=dst, send_sem=send_sem, recv_sem=recv_sem,
            device_id=self.sibling if device is None else device, device_id_type=MESH,
        )


class TwoStage:
    def __init__(self, plane, slot, send, recv):
        self.plane, self.slot, self.send, self.recv = plane, slot, send, recv

    def copy(self, part, first, second, axis, steps, number):
        one, two = self.plane.spot(part, first, second)
        z, x = (two, one) if part == 0 else (one, two)
        ref = self.slot(z, x, part)
        return self.plane.remote(ref, ref, self.send.at[number], self.recv.at[part, one * RING + two],
                                 self.plane.target(part, axis, steps))

    def wait(self, part, first, second):
        self.copy(part, first, second, 0, 1, 0).wait_recv()

    def start(self):
        number = 0
        for axis in (0, 1):
            for steps in (1, 3, 2):
                for part in (0, 1):
                    self.copy(part, 0, 0, axis, steps, number).start()
                    number += 1

    def forward(self):
        number = 12
        for first in (1, 3, 2):
            for part in (0, 1):
                self.wait(part, first, 0)
                for steps in (1, 3, 2):
                    self.copy(part, first, 0, 1, steps, number).start()
                    number += 1

    def finish(self):
        for first in (0, 1, 3, 2):
            for part in (0, 1):
                for second in (1, 3, 2):
                    self.wait(part, first, second)

    def drain(self):
        def body(number, carry):
            self.copy(0, 0, 0, 0, 1, number).wait_send()
            return carry

        lax.fori_loop(0, 30, body, 0)


DEPTH = 2
CHUNKS = ((0, 1, 2), (3, 4), (5, 6, 7))


class Bulk:
    def __init__(self, plane, buf, send, recv):
        self.plane, self.buf, self.send, self.recv = plane, buf, send, recv

    def copy(self, part, first, second, half, axis, steps, number):
        one, two = self.plane.spot(part, first, second)
        row = part * HALF + (one * RING + two) * LANE + half * 64
        ref = self.buf.at[pl.ds(multiple(row, 64), 64), :]
        return self.plane.remote(ref, ref, self.send.at[number], self.recv.at[part, one * RING + two, half],
                                 self.plane.target(part, axis, steps))

    def wait(self, first, second, half):
        for part in (0, 1):
            self.copy(part, first, second, half, 0, 1, 0).wait_recv()

    def sent(self, number):
        for k in range(4):
            self.copy(0, 0, 0, 0, 0, 1, number * 4 + k).wait_send()

    def put(self, number, plus, minus, axis):
        if number >= DEPTH:
            self.sent(number - DEPTH)
        for k, (what, steps) in enumerate(((plus, 1), (minus, 3))):
            for part in (0, 1):
                self.copy(part, *what, axis, steps, number * 4 + k * 2 + part).start()

    def spread(self, number, first, half):
        self.put(number, (first, 0, half), (first, 0, half), 1)

    def pass_on(self, number, first):
        self.wait(first, 3, 0)
        self.wait(first, 1, 1)
        self.put(number, (first, 3, 0), (first, 1, 1), 1)

    def round(self, number):
        if number < 2:
            self.put(number, (0, 0, number), (0, 0, number), 0)
        elif number < 4:
            self.spread(number, 0, number - 2)
        elif number == 4:
            self.wait(3, 0, 0)
            self.wait(1, 0, 1)
            self.put(number, (3, 0, 0), (1, 0, 1), 0)
        elif number == 5:
            self.wait(1, 0, 0)
            self.spread(number, 1, 0)
        elif number == 6:
            self.spread(number, 1, 1)
        elif number == 7:
            self.pass_on(number, 0)
        elif number == 8:
            self.spread(number, 3, 0)
        elif number == 9:
            self.wait(3, 0, 1)
            self.spread(number, 3, 1)
        elif number == 10:
            self.pass_on(number, 1)
        elif number in (11, 12):
            self.wait(2, 0, number - 11)
            self.spread(number, 2, number - 11)
        elif number == 13:
            self.pass_on(number, 3)
        elif number == 14:
            self.pass_on(number, 2)

    def complete(self, first):
        self.wait(first, 1, 0)
        self.wait(first, 3, 1)
        self.wait(first, 2, 0)
        self.wait(first, 2, 1)


def step_kernel(
    cot, xs, w, m, dout, nout, oout,
    mbuf, nbuf, nrow, wbuf, ubuf, gbuf, xin, slope, dbuf, bsend, brecv, bown, apart, aother, fpart, fother,
    eacc, ebf, qacc, obuf, own_sum, other_sum, sum_x, sum_z,
    lsem, sib_send, sib_recv, msend, mrecv, gsend, grecv, usend, urecv,
    asend, arecv, fsend, frecv, osem, orecv, nsem, nrecv, ssend, srecv,
):
    plane = Plane()
    y, z, x, core = plane.y, plane.z, plane.x, plane.core
    remote = plane.remote
    me = chip_of(z, x)
    own_spot = (1 - core) * (x * RING + z) + core * (z * RING + x)

    partners = [at(y, z, x + 1, core), at(y, z, x + 2, core), at(y, z, x + 3, core),
                at(y, z + 1, x, core), at(y, z + 2, x, core), at(y, z + 3, x, core),
                plane.sibling, at(ring(y, 1), z, x, core), at(ring(y, 3), z, x, core)]
    load_x = pltpu.make_async_copy(xs.at[0], xin, lsem.at[0])
    load_x.start()
    barrier = pltpu.get_barrier_semaphore()
    for partner in partners:
        pl.semaphore_signal(barrier, 1, device_id=partner, device_id_type=MESH)

    own_m = mbuf.at[pl.ds(multiple(core * HALF + own_spot * LANE, LANE), LANE), :]

    def own_columns(k, core_at):
        return pl.ds(multiple((2 * k + core_at) * LANE, LANE), LANE)

    def load_own(k, carry):
        lanes = pl.ds(multiple(k * LANE, LANE), LANE)
        pltpu.make_async_copy(m.at[0, :, own_columns(k, core)], own_m.at[:, lanes], lsem.at[1]).start()
        pltpu.make_async_copy(w.at[0, :, own_columns(k, core)], wbuf.at[core, :, lanes], lsem.at[2]).start()
        return carry

    lax.fori_loop(0, CHIPS, load_own, 0)
    pl.semaphore_wait(barrier, len(partners))

    def give_sibling(k, carry):
        lanes = pl.ds(multiple(k * LANE, LANE), LANE)
        remote(m.at[0, :, own_columns(k, 1 - core)], own_m.at[:, lanes], sib_send.at[0], sib_recv.at[0]).start()
        remote(w.at[0, :, own_columns(k, 1 - core)], wbuf.at[core, :, lanes],
               sib_send.at[1], sib_recv.at[1]).start()
        return carry

    lax.fori_loop(0, CHIPS, give_sibling, 0)

    load_x.wait()
    values = xin[...].reshape(TOKENS, LANE).astype(F32)
    sigmoid_val = jax.nn.sigmoid(values)
    slope[...] = sigmoid_val * (1.0 + values * (1.0 - sigmoid_val))
    gated = (values * sigmoid_val).astype(BF).astype(F32)
    gbuf[core, pl.ds(multiple(own_spot * LANE, LANE), LANE), :] = jnp.transpose(gated).astype(BF)

    def g_slot(z_at, x_at, part):
        spot = (1 - core) * (x_at * RING + z_at) + core * (z_at * RING + x_at)
        return gbuf.at[core, pl.ds(multiple(spot * LANE + part * 64, 64), 64), :]

    def u_slot(z_at, x_at, part):
        return ubuf.at[pl.ds(part * LANE, LANE), pl.ds(multiple((z_at * RING + x_at) * LANE, LANE), LANE)]

    bulk = Bulk(plane, mbuf, msend, mrecv)
    gather_g = TwoStage(plane, g_slot, gsend, grecv)
    gather_u = TwoStage(plane, u_slot, usend, urecv)
    gather_g.start()

    own_u = ubuf.at[:, pl.ds(multiple(me * LANE, LANE), LANE)]

    def from_above():
        return remote(dbuf, own_u, sib_send.at[3], sib_recv.at[3], at(ring(y, 3), z, x, core))

    def chain():
        @pl.when(y == RING - 1)
        def _():
            for micro in range(2):
                pltpu.make_async_copy(
                    cot.at[micro],
                    ubuf.at[pl.ds(micro * LANE, LANE), pl.ds(multiple(me * LANE, LANE), LANE)],
                    lsem.at[3]).start()
            pltpu.make_async_copy(own_u, own_u, lsem.at[3]).wait()

        @pl.when(y < RING - 1)
        def _():
            from_above().wait_recv()

        gather_u.start()
        gather_u.forward()
        pltpu.make_async_copy(wbuf.at[core], wbuf.at[core], lsem.at[2]).wait()
        remote(wbuf.at[core], wbuf.at[core], sib_send.at[1], sib_recv.at[1]).wait_recv()
        gather_u.finish()
        full = ubuf[...]
        bsend[...] = lax.dot_general(full, wbuf[1 - core], NT, preferred_element_type=F32)
        give = remote(bsend, brecv, sib_send.at[2], sib_recv.at[2])
        give.start()
        bown[...] = lax.dot_general(full, wbuf[core], NT, preferred_element_type=F32)
        give.wait()
        back = bown[...] + brecv[...]
        upstream = ubuf[:, pl.ds(multiple(me * LANE, LANE), LANE)].astype(F32)
        dbuf[...] = (upstream + slope[...] * back).astype(BF)

        @pl.when(y > 0)
        def _():
            from_above().start()

        for micro in range(2):
            pltpu.make_async_copy(
                dbuf.at[pl.ds(micro * LANE, LANE), :], dout.at[0, micro], lsem.at[4]).start()

    pltpu.make_async_copy(own_m, own_m, lsem.at[1]).wait()
    remote(own_m, own_m, sib_send.at[0], sib_recv.at[0]).wait_recv()

    def front(index, carry):
        @pl.when(index == RING - 1 - y)
        def _():
            chain()

        for which, rounds in enumerate(CHUNKS):
            @pl.when(index == which)
            def _(which=which, rounds=rounds):
                if which == 1:
                    gather_g.forward()
                for number in rounds:
                    bulk.round(number)
        return carry

    lax.fori_loop(0, RING, front, 0)

    def share(part):
        return remote(gbuf.at[part], gbuf.at[part], sib_send.at[4], sib_recv.at[4])

    gather_g.finish()
    share(core).start()

    share(1 - core).wait_recv()
    sums = jnp.zeros((8, LANE), F32)
    for part in (0, 1):
        one, two = plane.own(part)
        spot = one * RING + two
        grad = lax.dot_general(
            gbuf[part, pl.ds(multiple(spot * LANE, LANE), LANE), :], ubuf[...], NN,
            preferred_element_type=F32)
        old = mbuf[pl.ds(multiple(part * HALF + spot * LANE, LANE), LANE), :].astype(F32)
        fresh = (0.95 * old + grad).astype(BF)
        nrow[pl.ds(part * LANE, LANE), :] = fresh
        wide = fresh.astype(F32)
        square = wide * wide
        for k in range(CHIPS):
            sums = sums + jnp.sum(
                square[:, k * LANE:(k + 1) * LANE].reshape(16, 8, LANE), axis=0)
    own_sum[...] = sums
    swap = remote(own_sum, other_sum, sib_send.at[5], sib_recv.at[5])
    swap.start()

    def give_rows(buf, out, sem, recv):
        def body(k, carry):
            lanes = pl.ds(multiple(k * LANE, LANE), LANE)
            pltpu.make_async_copy(
                buf.at[pl.ds(multiple(core * LANE, LANE), LANE), lanes],
                out.at[0, :, own_columns(k, core)], sem.at[0]).start()
            remote(buf.at[pl.ds(multiple((1 - core) * LANE, LANE), LANE), lanes],
                   out.at[0, :, own_columns(k, core)], sem.at[1], recv).start()
            return carry

        lax.fori_loop(0, CHIPS, body, 0)

    def wait_rows(buf, sem, recv):
        half = buf.at[pl.ds(0, LANE), :]
        pltpu.make_async_copy(half, half, sem.at[0]).wait()
        both = remote(half, half, sem.at[1], recv)
        both.wait_send()
        both.wait_recv()

    give_rows(nrow, nout, nsem, nrecv)

    def to_ring(buf, axis, steps, own):
        return remote(buf.at[own], buf.at[own], ssend.at[axis, steps - 1], srecv.at[axis, own],
                      plane.target(0, axis, steps))

    def start_ring(buf, axis, own, value):
        buf[own] = value
        for steps in (1, 2, 3):
            to_ring(buf, axis, steps, own).start()

    def wait_ring(buf, axis, own):
        for steps in (1, 2, 3):
            to_ring(buf, axis, steps, ring(own, steps)).wait_recv()
        return buf[0] + buf[1] + buf[2] + buf[3]

    def group_rows(index, part):
        first = plane.spot(part, OFFSETS[index], 0)[0]
        return part, multiple(first * 512, 512)

    def a_copy(slot):
        return remote(apart.at[slot], aother.at[slot], asend.at[slot], arecv.at[slot])

    def f_copy(slot):
        return remote(fpart.at[slot], fother.at[slot], fsend.at[slot], frecv.at[slot])

    def build(index):
        for part in (0, 1):
            part, start = group_rows(index, part)
            rows = pl.ds(part * HALF + start, 512)
            grad = lax.dot_general(gbuf[part, pl.ds(start, 512), :], ubuf[...], NN,
                                   preferred_element_type=F32)
            nbuf[rows, :] = (0.95 * mbuf[rows, :].astype(F32) + grad).astype(BF)

    def gram(index):
        for part in (0, 1):
            part, start = group_rows(index, part)
            rows = pl.ds(part * HALF + start, 512)
            product = lax.dot_general(nrow[...], nbuf[rows, :], NT, preferred_element_type=F32)
            apart[index * 2 + part] = (product * inverse).astype(BF)
            a_copy(index * 2 + part).start()

    def cubic(index):
        for part in (0, 1):
            part, start = group_rows(index, part)
            rows = pl.ds(part * HALF + start, 512)
            slot = index * 2 + part
            a_copy(slot).wait_recv()
            whole = (apart[slot].astype(F32) + aother[slot].astype(F32)).astype(BF)
            product = lax.dot_general(whole, nbuf[rows, :], NN, preferred_element_type=F32)
            if slot == 0:
                eacc[...] = product
            else:
                eacc[...] += product

    bulk.round(8)
    swap.wait()
    chip_sum = own_sum[...] + other_sum[...]
    start_ring(sum_x, 0, x, chip_sum)
    chip_norm = jnp.sqrt(jnp.maximum(jnp.sum(chip_sum), 1e-30))
    inverse = 1.0 / chip_norm
    bulk.complete(OFFSETS[0])
    build(0)
    bulk.round(9)
    gram(0)
    bulk.round(10)
    cubic(0)
    bulk.round(11)
    start_ring(sum_z, 1, z, wait_ring(sum_x, 0, x))
    bulk.complete(OFFSETS[1])
    build(1)
    bulk.round(12)
    gram(1)
    bulk.round(13)
    cubic(1)
    bulk.complete(OFFSETS[2])
    build(2)
    bulk.round(14)
    gram(2)
    cubic(2)
    sum_squares = jnp.sum(wait_ring(sum_z, 1, z))
    scaling = 0.4 / jnp.sqrt(float(WIDTH) * (sum_squares / float(WIDTH * WIDTH) + 1e-06))
    bulk.complete(OFFSETS[3])
    build(3)
    gram(3)
    cubic(3)
    ebf[...] = (((eacc[...] * scaling) * scaling) * (scaling * chip_norm)).astype(BF)

    def back_part(slot):
        product = lax.dot_general(ebf[...], nbuf[pl.ds(slot * 1024, 1024), :], NT, preferred_element_type=F32)
        fpart[slot] = (product * scaling).astype(BF)
        f_copy(slot).start()

    def quintic(slot):
        f_copy(slot).wait_recv()
        whole = (fpart[slot].astype(F32) + fother[slot].astype(F32)).astype(BF)
        product = lax.dot_general(whole, nbuf[pl.ds(slot * 1024, 1024), :], NN, preferred_element_type=F32)
        if slot == 0:
            qacc[...] = product
        else:
            qacc[...] += product

    for slot in range(4):
        back_part(slot)
    for slot in range(4):
        quintic(slot)
    scaled = (nrow[...].astype(F32) * scaling).astype(BF).astype(F32)
    mixed = (quintic_a * scaled + quintic_b * ebf[...].astype(F32)
             + quintic_c * (qacc[...] * scaling))
    obuf[...] = (math.sqrt(WIDTH) * mixed).astype(BF)
    give_rows(obuf, oout, osem, orecv)

    @pl.when(y > 0)
    def _():
        from_above().wait_send()

    pltpu.make_async_copy(dbuf, dbuf, lsem.at[4]).wait()
    remote(own_m, own_m, sib_send.at[0], sib_recv.at[0]).wait_send()
    remote(wbuf.at[core], wbuf.at[core], sib_send.at[1], sib_recv.at[1]).wait_send()
    share(core).wait_send()
    for number in range(15 - DEPTH, 15):
        bulk.sent(number)
    gather_g.drain()
    gather_u.drain()
    for axis, buf in enumerate((sum_x, sum_z)):
        for steps in (1, 2, 3):
            to_ring(buf, axis, steps, 0).wait_send()
    for slot in range(8):
        a_copy(slot).wait_send()
    for slot in range(4):
        f_copy(slot).wait_send()
    wait_rows(nrow, nsem, nrecv)
    wait_rows(obuf, osem, orecv)


def per_device(cotangent, stashed_inputs, weights, momentum):
    anywhere = pl.BlockSpec(memory_space=pl.ANY)
    sem = pltpu.SemaphoreType.DMA
    scratch = [
        pltpu.VMEM((WIDTH, HALF), BF),
        pltpu.VMEM((WIDTH, HALF), BF),
        pltpu.VMEM((ROWS, HALF), BF),
        pltpu.VMEM((2, LANE, HALF), BF),
        pltpu.VMEM((TOKENS, HALF), BF),
        pltpu.VMEM((2, HALF, TOKENS), BF),
        pltpu.VMEM((2, LANE, LANE), BF),
        pltpu.VMEM((TOKENS, LANE), F32),
        pltpu.VMEM((TOKENS, LANE), BF),
        pltpu.VMEM((TOKENS, LANE), F32),
        pltpu.VMEM((TOKENS, LANE), F32),
        pltpu.VMEM((TOKENS, LANE), F32),
        pltpu.VMEM((8, ROWS, 512), BF),
        pltpu.VMEM((8, ROWS, 512), BF),
        pltpu.VMEM((4, ROWS, 1024), BF),
        pltpu.VMEM((4, ROWS, 1024), BF),
        pltpu.VMEM((ROWS, HALF), F32),
        pltpu.VMEM((ROWS, HALF), BF),
        pltpu.VMEM((ROWS, HALF), F32),
        pltpu.VMEM((ROWS, HALF), BF),
        pltpu.VMEM((8, LANE), F32),
        pltpu.VMEM((8, LANE), F32),
        pltpu.VMEM((RING, 8, LANE), F32),
        pltpu.VMEM((RING, 8, LANE), F32),
        sem((5,)),
        sem((6,)),
        sem((6,)),
        sem((60,)),
        sem((2, CHIPS, 2)),
        sem((30,)),
        sem((2, CHIPS)),
        sem((30,)),
        sem((2, CHIPS)),
        sem((8,)),
        sem((8,)),
        sem((4,)),
        sem((4,)),
        sem((2,)),
        sem,
        sem((2,)),
        sem,
        sem((2, 3)),
        sem((2, RING)),
    ]
    return pl.pallas_call(
        step_kernel,
        out_shape=(
            jax.ShapeDtypeStruct(stashed_inputs.shape, BF),
            jax.ShapeDtypeStruct(momentum.shape, BF),
            jax.ShapeDtypeStruct(momentum.shape, BF),
        ),
        in_specs=[anywhere] * 4,
        out_specs=(anywhere, anywhere, anywhere),
        scratch_shapes=scratch,
        compiler_params=pltpu.CompilerParams(
            collective_id=0, has_side_effects=True, vmem_limit_bytes=60 * 1024 * 1024),
        cost_estimate=pl.CostEstimate(
            flops=22 * 10**9, bytes_accessed=6 * 2**20, transcendentals=32768),
    )(cotangent, stashed_inputs, weights, momentum)


def solution(mesh):
    in_specs = (
        P(None, None, "dp"),
        P("pipe", None, None, "dp"),
        P("pipe", "dp", None),
        P("pipe", "dp", None),
    )
    out_specs = (P("pipe", None, None, "dp"), P("pipe", "dp", None), P("pipe", "dp", None))
    return jax.shard_map(
        per_device, mesh=mesh, in_specs=in_specs, out_specs=out_specs, check_vma=False
    )
```

time: 518 us -> 146 us (0.28)
  waiting for transfers between devices: 342 us -> 0 us
  Pallas kernels: 0 us -> 140 us
  matrix products: 84.3 us -> 0 us
  blocking collectives: 63.1 us -> 0 us
  between operations: 15 us -> 0.64 us
  other arithmetic: 7.25 us -> 0 us
  starting transfers between devices: 5.41 us -> 0 us
    all_gather x6 -> x0, waiting for transfers between devices: 329 us -> none  [the longest x5 216 us: per_device(): full_grad = lax.all_gather(upstream, 'dp', axis=1, tiled=True)]
    pallas_call x0 -> x1, Pallas kernels: none -> 140 us  [per_device(): pl.pallas_call(step_kernel, out_shape=(jax.ShapeDtypeStruct(stashed_input...]
    dot_general x12 -> x0, matrix products: 84.3 us -> none  [the longest x1 32.8 us: per_device(): jnp.dot(back_rows, whole_matrix, preferred_element_type=jnp.float32)]
    psum x1 -> x0, blocking collectives: 63.1 us -> none  [per_device(): sum_squares = lax.psum(jnp.sum(fresh32 * fresh32), 'dp')]
    ppermute x4 -> x0, waiting for transfers between devices: 13.4 us -> none  [from_behind(): lax.ppermute(value, axis, [(source, source + steps) for source in range(l...]
  transfers between devices with their start and end apart: 10 -> 0, of which waited for: 10 -> 0; matrix products, arithmetic and copies ran while one was open for 2% -> 0% of each run, Pallas kernels for 0% -> 0%
where the time goes in v2:
time: 146 us
  Pallas kernels  140 us (96%)
  local copies, waits for them, and re-layouts  4.82 us (3%)
    pallas_call x1, Pallas kernels, per_device(): pl.pallas_call(step_kernel, out_shape=(jax.ShapeDtypeStruct(stashed_input...  140 us
    unnamed x5, local copies, waits for them, and re-layouts  4.82 us

profile of v2, /device:TPU:1, one launch (start us, length us, event | category | flops | bytes accessed | tf_op | source)
XLA Modules:
  0.0 145.9 jit_solution(7196072001837369347)
XLA Ops:
  0.6 140.4 %shard_map.67 = (bf16[1,2,128,128]{3,2,1,0:T(8,128)(2,1)}, bf16[1,128,4096]{2,1,0:T(8,128)(2,1)}, bf16[1,128,4096]{2,1,0:T(8,128)(2,1)}) custom-call(bf16[2,128,128]{2,1,0:T(8,128)(2,1)} %cot.1, bf16[1,2,128,128]{3,2,1,0:T(8,128)(2,1)} %xs.1, bf16[1,128,4096]{2,1,0:T(8,128)(2,1)} %w.1, bf16[1,128,4096]{2,1,0:T(8,128)(2,1)} %m.1), custom_call_target="tpu_custom_call" | custom-call | flops 22000001024 | bytes 6291456 | tf_op jit(solution)/shard_map/pallas_call | solution.py:550
  141.1 1.5 %copy.10 = bf16[1,2,128,128]{3,2,1,0:T(8,128)(2,1)} copy(bf16[1,2,128,128]{3,2,1,0:T(8,128)(2,1)} %get-tuple-element.6) | data formatting | bytes 131072
  142.6 0.0 copy-start
  142.6 2.4 %copy.11 = bf16[1,128,4096]{2,1,0:T(8,128)(2,1)} copy(bf16[1,128,4096]{2,1,0:T(8,128)(2,1)} %get-tuple-element.7) | data formatting | bytes 2097152
  144.9 0.0 copy-done
  144.9 1.0 copy.12
Async XLA Ops:
  142.6 2.4 %copy-start = (bf16[1,128,4096]{2,1,0:T(8,128)(2,1)S(1)}, bf16[1,128,4096]{2,1,0:T(8,128)(2,1)}, u32[]{:S(2)}) copy-start(bf16[1,128,4096]{2,1,0:T(8,128)(2,1)} %get-tuple-element.8) | copy-start | bytes 3145732

commit v3 on v2

--- a/solution.py
+++ b/solution.py
@@ -119,7 +119,8 @@
 
 
 DEPTH = 2
-CHUNKS = ((0, 1, 2), (3, 4), (5, 6, 7))
+CHUNKS = ((0, 1), (2, 3, 4), (5, 6))
+EXTRA = {3: (0, 1), 2: (2, 3), 1: (5,), 0: (7, 8)}
 
 
 class Bulk:
@@ -197,7 +198,7 @@
 def step_kernel(
     cot, xs, w, m, dout, nout, oout,
     mbuf, nbuf, nrow, wbuf, ubuf, gbuf, xin, slope, dbuf, bsend, brecv, bown, apart, aother, fpart, fother,
-    eacc, ebf, qacc, obuf, own_sum, other_sum, sum_x, sum_z,
+    eacc, ebf, fwhole, stage, own_sum, other_sum, sum_x, sum_z,
     lsem, sib_send, sib_recv, msend, mrecv, gsend, grecv, usend, urecv,
     asend, arecv, fsend, frecv, osem, orecv, nsem, nrecv, ssend, srecv,
 ):
@@ -211,33 +212,60 @@
                 at(y, z + 1, x, core), at(y, z + 2, x, core), at(y, z + 3, x, core),
                 plane.sibling, at(ring(y, 1), z, x, core), at(ring(y, 3), z, x, core)]
     load_x = pltpu.make_async_copy(xs.at[0], xin, lsem.at[0])
-    load_x.start()
+    own_u = ubuf.at[:, pl.ds(multiple(me * LANE, LANE), LANE)]
     barrier = pltpu.get_barrier_semaphore()
     for partner in partners:
         pl.semaphore_signal(barrier, 1, device_id=partner, device_id_type=MESH)
 
+    @pl.when(y == RING - 1)
+    def _():
+        for micro in range(2):
+            pltpu.make_async_copy(
+                cot.at[micro],
+                ubuf.at[pl.ds(micro * LANE, LANE), pl.ds(multiple(me * LANE, LANE), LANE)],
+                lsem.at[3]).start()
+
+    load_x.start()
     own_m = mbuf.at[pl.ds(multiple(core * HALF + own_spot * LANE, LANE), LANE), :]
 
-    def own_columns(k, core_at):
-        return pl.ds(multiple((2 * k + core_at) * LANE, LANE), LANE)
-
-    def load_own(k, carry):
-        lanes = pl.ds(multiple(k * LANE, LANE), LANE)
-        pltpu.make_async_copy(m.at[0, :, own_columns(k, core)], own_m.at[:, lanes], lsem.at[1]).start()
-        pltpu.make_async_copy(w.at[0, :, own_columns(k, core)], wbuf.at[core, :, lanes], lsem.at[2]).start()
-        return carry
-
-    lax.fori_loop(0, CHIPS, load_own, 0)
+    def load_rows(src, at_stage, which):
+        for half in (0, 1):
+            pltpu.make_async_copy(src.at[0, :, pl.ds(half * HALF, HALF)],
+                                  stage.at[at_stage, pl.ds(half * LANE, LANE), :], lsem.at[which]).start()
+
+    def given(at_stage, dst, which):
+        return remote(stage.at[at_stage + 1, pl.ds(0, LANE), :], dst, sib_send.at[which], sib_recv.at[which])
+
+    def split_rows(at_stage, dst, which, own_which):
+        whole = stage.at[at_stage]
+        pltpu.make_async_copy(whole, whole, lsem.at[own_which]).wait()
+        for k in range(CHIPS):
+            half, lanes = k // 8, pl.ds(k * LANE, LANE)
+            for mine in (1, 0):
+                which_core = core if mine else 1 - core
+                source = pl.ds(multiple((2 * (k % 8) + which_core) * LANE, LANE), LANE)
+                piece = stage[at_stage, pl.ds(half * LANE, LANE), source]
+                if mine:
+                    dst[:, lanes] = piece
+                else:
+                    stage[at_stage + 1, pl.ds(0, LANE), lanes] = piece
+        given(at_stage, dst, which).start()
+
+    load_rows(m, 0, 1)
+    load_rows(w, 2, 2)
     pl.semaphore_wait(barrier, len(partners))
 
-    def give_sibling(k, carry):
-        lanes = pl.ds(multiple(k * LANE, LANE), LANE)
-        remote(m.at[0, :, own_columns(k, 1 - core)], own_m.at[:, lanes], sib_send.at[0], sib_recv.at[0]).start()
-        remote(w.at[0, :, own_columns(k, 1 - core)], wbuf.at[core, :, lanes],
-               sib_send.at[1], sib_recv.at[1]).start()
-        return carry
-
-    lax.fori_loop(0, CHIPS, give_sibling, 0)
+    def u_slot(z_at, x_at, part):
+        return ubuf.at[pl.ds(part * LANE, LANE), pl.ds(multiple((z_at * RING + x_at) * LANE, LANE), LANE)]
+
+    gather_u = TwoStage(plane, u_slot, usend, urecv)
+
+    @pl.when(y == RING - 1)
+    def _():
+        pltpu.make_async_copy(own_u, own_u, lsem.at[3]).wait()
+        gather_u.start()
+
+    split_rows(0, own_m, 0, 1)
 
     load_x.wait()
     values = xin[...].reshape(TOKENS, LANE).astype(F32)
@@ -246,42 +274,56 @@
     gated = (values * sigmoid_val).astype(BF).astype(F32)
     gbuf[core, pl.ds(multiple(own_spot * LANE, LANE), LANE), :] = jnp.transpose(gated).astype(BF)
 
+    def load_weights():
+        split_rows(2, wbuf.at[core], 1, 2)
+
     def g_slot(z_at, x_at, part):
         spot = (1 - core) * (x_at * RING + z_at) + core * (z_at * RING + x_at)
         return gbuf.at[core, pl.ds(multiple(spot * LANE + part * 64, 64), 64), :]
 
-    def u_slot(z_at, x_at, part):
-        return ubuf.at[pl.ds(part * LANE, LANE), pl.ds(multiple((z_at * RING + x_at) * LANE, LANE), LANE)]
-
     bulk = Bulk(plane, mbuf, msend, mrecv)
     gather_g = TwoStage(plane, g_slot, gsend, grecv)
-    gather_u = TwoStage(plane, u_slot, usend, urecv)
-    gather_g.start()
-
-    own_u = ubuf.at[:, pl.ds(multiple(me * LANE, LANE), LANE)]
 
     def from_above():
         return remote(dbuf, own_u, sib_send.at[3], sib_recv.at[3], at(ring(y, 3), z, x, core))
 
+    def own_rows_here():
+        given(0, own_m, 0).wait()
+
+    def go(number):
+        taken = [at_y for at_y, rounds in EXTRA.items() if number in rounds]
+        if not taken:
+            bulk.round(number)
+        else:
+            @pl.when(y != taken[0])
+            def _():
+                bulk.round(number)
+
     def chain():
-        @pl.when(y == RING - 1)
-        def _():
-            for micro in range(2):
-                pltpu.make_async_copy(
-                    cot.at[micro],
-                    ubuf.at[pl.ds(micro * LANE, LANE), pl.ds(multiple(me * LANE, LANE), LANE)],
-                    lsem.at[3]).start()
-            pltpu.make_async_copy(own_u, own_u, lsem.at[3]).wait()
-
         @pl.when(y < RING - 1)
         def _():
             from_above().wait_recv()
-
-        gather_u.start()
+            gather_u.start()
+
         gather_u.forward()
-        pltpu.make_async_copy(wbuf.at[core], wbuf.at[core], lsem.at[2]).wait()
-        remote(wbuf.at[core], wbuf.at[core], sib_send.at[1], sib_recv.at[1]).wait_recv()
+        for at_y, rounds in EXTRA.items():
+            @pl.when(y == at_y)
+            def _(rounds=rounds, at_y=at_y):
+                if at_y == RING - 1:
+                    gather_g.start()
+                    own_rows_here()
+                    load_weights()
+                for number in rounds:
+                    bulk.round(number)
+
         gather_u.finish()
+
+        @pl.when(y > 0)
+        def _():
+            back_product()
+
+    def back_product():
+        given(2, wbuf.at[core], 1).wait()
         full = ubuf[...]
         bsend[...] = lax.dot_general(full, wbuf[1 - core], NT, preferred_element_type=F32)
         give = remote(bsend, brecv, sib_send.at[2], sib_recv.at[2])
@@ -300,9 +342,6 @@
             pltpu.make_async_copy(
                 dbuf.at[pl.ds(micro * LANE, LANE), :], dout.at[0, micro], lsem.at[4]).start()
 
-    pltpu.make_async_copy(own_m, own_m, lsem.at[1]).wait()
-    remote(own_m, own_m, sib_send.at[0], sib_recv.at[0]).wait_recv()
-
     def front(index, carry):
         @pl.when(index == RING - 1 - y)
         def _():
@@ -311,13 +350,21 @@
         for which, rounds in enumerate(CHUNKS):
             @pl.when(index == which)
             def _(which=which, rounds=rounds):
+                if which == 0:
+                    @pl.when(y < RING - 1)
+                    def _():
+                        gather_g.start()
+                        own_rows_here()
+                        load_weights()
                 if which == 1:
                     gather_g.forward()
                 for number in rounds:
-                    bulk.round(number)
+                    go(number)
         return carry
 
     lax.fori_loop(0, RING, front, 0)
+
+    go(7)
 
     def share(part):
         return remote(gbuf.at[part], gbuf.at[part], sib_send.at[4], sib_recv.at[4])
@@ -345,17 +392,11 @@
     swap = remote(own_sum, other_sum, sib_send.at[5], sib_recv.at[5])
     swap.start()
 
-    def give_rows(buf, out, sem, recv):
-        def body(k, carry):
-            lanes = pl.ds(multiple(k * LANE, LANE), LANE)
-            pltpu.make_async_copy(
-                buf.at[pl.ds(multiple(core * LANE, LANE), LANE), lanes],
-                out.at[0, :, own_columns(k, core)], sem.at[0]).start()
-            remote(buf.at[pl.ds(multiple((1 - core) * LANE, LANE), LANE), lanes],
-                   out.at[0, :, own_columns(k, core)], sem.at[1], recv).start()
-            return carry
-
-        lax.fori_loop(0, CHIPS, body, 0)
+    def give_rows(buf, out, sem, recv, lanes=pl.ds(0, HALF)):
+        pltpu.make_async_copy(
+            buf.at[pl.ds(multiple(core * LANE, LANE), LANE), lanes], out.at[core, :, lanes], sem.at[0]).start()
+        remote(buf.at[pl.ds(multiple((1 - core) * LANE, LANE), LANE), lanes], out.at[core, :, lanes],
+               sem.at[1], recv).start()
 
     def wait_rows(buf, sem, recv):
         half = buf.at[pl.ds(0, LANE), :]
@@ -419,84 +460,164 @@
             else:
                 eacc[...] += product
 
-    bulk.round(8)
+    def small(second):
+        parts = []
+        for part in (0, 1):
+            first, last = plane.spot(part, OFFSETS[3], second)
+            start = multiple((first * RING + last) * LANE, LANE)
+            rows = pl.ds(part * HALF + start, LANE)
+            grad = lax.dot_general(gbuf[part, pl.ds(start, LANE), :], ubuf[...], NN,
+                                   preferred_element_type=F32)
+            fresh = (0.95 * mbuf[rows, :].astype(F32) + grad).astype(BF)
+            nbuf[rows, :] = fresh
+            stage[second, pl.ds(part * LANE, LANE), :] = fresh
+        product = lax.dot_general(nrow[...], stage[second], NT, preferred_element_type=F32)
+        slot, lanes = 6 + second // 2, pl.ds((second % 2) * ROWS, ROWS)
+        apart[slot, :, lanes] = (product * inverse).astype(BF)
+        small_copy(second).start()
+
+    def small_copy(second):
+        slot, lanes = 6 + second // 2, pl.ds((second % 2) * ROWS, ROWS)
+        return remote(apart.at[slot, :, lanes], aother.at[slot, :, lanes],
+                      asend.at[6 + second], arecv.at[6 + second])
+
+    def small_cubic(second):
+        small_copy(second).wait_recv()
+        slot, lanes = 6 + second // 2, pl.ds((second % 2) * ROWS, ROWS)
+        whole = (apart[slot, :, lanes].astype(F32) + aother[slot, :, lanes].astype(F32)).astype(BF)
+        eacc[...] += lax.dot_general(whole, stage[second], NN, preferred_element_type=F32)
+
+    def settle():
+        @pl.when(y > 0)
+        def _():
+            from_above().wait_send()
+
+        pltpu.make_async_copy(dbuf, dbuf, lsem.at[4]).wait()
+        share(core).wait_send()
+        gather_g.drain()
+        gather_u.drain()
+        for steps in (1, 2, 3):
+            to_ring(sum_x, 0, steps, 0).wait_send()
+        for slot in range(4):
+            a_copy(slot).wait_send()
+        small_copy(0).wait_send()
+        small_copy(1).wait_send()
+        wait_rows(nrow, nsem, nrecv)
+
+    go(8)
     swap.wait()
     chip_sum = own_sum[...] + other_sum[...]
     start_ring(sum_x, 0, x, chip_sum)
     chip_norm = jnp.sqrt(jnp.maximum(jnp.sum(chip_sum), 1e-30))
     inverse = 1.0 / chip_norm
     bulk.complete(OFFSETS[0])
+    go(9)
     build(0)
-    bulk.round(9)
     gram(0)
-    bulk.round(10)
+
+    @pl.when(y == 0)
+    def _():
+        back_product()
+
+    go(10)
     cubic(0)
-    bulk.round(11)
+    go(11)
     start_ring(sum_z, 1, z, wait_ring(sum_x, 0, x))
     bulk.complete(OFFSETS[1])
     build(1)
-    bulk.round(12)
+    go(12)
     gram(1)
-    bulk.round(13)
+    go(13)
     cubic(1)
+    small(0)
+    go(14)
+    bulk.wait(2, 1, 0)
+    small(1)
+    small_cubic(0)
+    bulk.wait(2, 3, 1)
+    small(3)
+    small_cubic(1)
+    settle()
     bulk.complete(OFFSETS[2])
     build(2)
-    bulk.round(14)
     gram(2)
-    cubic(2)
+    small_cubic(3)
     sum_squares = jnp.sum(wait_ring(sum_z, 1, z))
     scaling = 0.4 / jnp.sqrt(float(WIDTH) * (sum_squares / float(WIDTH * WIDTH) + 1e-06))
-    bulk.complete(OFFSETS[3])
-    build(3)
-    gram(3)
-    cubic(3)
+    bulk.wait(2, 2, 0)
+    bulk.wait(2, 2, 1)
+    small(2)
+    cubic(2)
+    small_cubic(2)
     ebf[...] = (((eacc[...] * scaling) * scaling) * (scaling * chip_norm)).astype(BF)
+
+    for slot in (4, 5):
+        a_copy(slot).wait_send()
+    small_copy(2).wait_send()
+    small_copy(3).wait_send()
+    for steps in (1, 2, 3):
+        to_ring(sum_z, 1, steps, 0).wait_send()
+    for number in range(15 - DEPTH, 15):
+        bulk.sent(number)
 
     def back_part(slot):
         product = lax.dot_general(ebf[...], nbuf[pl.ds(slot * 1024, 1024), :], NT, preferred_element_type=F32)
         fpart[slot] = (product * scaling).astype(BF)
         f_copy(slot).start()
 
-    def quintic(slot):
+    def back_whole(slot):
         f_copy(slot).wait_recv()
-        whole = (fpart[slot].astype(F32) + fother[slot].astype(F32)).astype(BF)
-        product = lax.dot_general(whole, nbuf[pl.ds(slot * 1024, 1024), :], NN, preferred_element_type=F32)
-        if slot == 0:
-            qacc[...] = product
-        else:
-            qacc[...] += product
-
+        fwhole[:, pl.ds(slot * 1024, 1024)] = (
+            fpart[slot].astype(F32) + fother[slot].astype(F32)).astype(BF)
+
+    obuf = stage.at[0]
     for slot in range(4):
         back_part(slot)
-    for slot in range(4):
-        quintic(slot)
-    scaled = (nrow[...].astype(F32) * scaling).astype(BF).astype(F32)
-    mixed = (quintic_a * scaled + quintic_b * ebf[...].astype(F32)
-             + quintic_c * (qacc[...] * scaling))
-    obuf[...] = (math.sqrt(WIDTH) * mixed).astype(BF)
-    give_rows(obuf, oout, osem, orecv)
-
-    @pl.when(y > 0)
-    def _():
-        from_above().wait_send()
-
-    pltpu.make_async_copy(dbuf, dbuf, lsem.at[4]).wait()
-    remote(own_m, own_m, sib_send.at[0], sib_recv.at[0]).wait_send()
-    remote(wbuf.at[core], wbuf.at[core], sib_send.at[1], sib_recv.at[1]).wait_send()
-    share(core).wait_send()
-    for number in range(15 - DEPTH, 15):
-        bulk.sent(number)
-    gather_g.drain()
-    gather_u.drain()
-    for axis, buf in enumerate((sum_x, sum_z)):
-        for steps in (1, 2, 3):
-            to_ring(buf, axis, steps, 0).wait_send()
-    for slot in range(8):
-        a_copy(slot).wait_send()
+    for slot in range(3):
+        back_whole(slot)
+    for cut in range(4):
+        lanes = pl.ds(cut * 512, 512)
+        product = lax.dot_general(fwhole[:, pl.ds(0, 3072)], nbuf[pl.ds(0, 3072), lanes], NN,
+                                  preferred_element_type=F32)
+        if cut == 0:
+            back_whole(3)
+        product = product + lax.dot_general(
+            fwhole[:, pl.ds(3072, 1024)], nbuf[pl.ds(3072, 1024), lanes], NN, preferred_element_type=F32)
+        scaled = (nrow[:, lanes].astype(F32) * scaling).astype(BF).astype(F32)
+        mixed = (quintic_a * scaled + quintic_b * ebf[:, lanes].astype(F32)
+                 + quintic_c * (product * scaling))
+        obuf[:, lanes] = (math.sqrt(WIDTH) * mixed).astype(BF)
+        give_rows(obuf, oout, osem, orecv, lanes)
+
     for slot in range(4):
         f_copy(slot).wait_send()
-    wait_rows(nrow, nsem, nrecv)
     wait_rows(obuf, osem, orecv)
+
+
+def copy_kernel(grads, fresh, update, grads_out, fresh_out, update_out, small, halves, wholes, come, leave):
+    grads_in = pltpu.make_async_copy(grads, small, come.at[4])
+    grads_away = pltpu.make_async_copy(small, grads_out, leave.at[4])
+    arriving, leaving = [], []
+    for which, (src, dst) in enumerate(((fresh, fresh_out), (update, update_out))):
+        for k in range(2):
+            rows, number = pl.ds(k * 64, 64), which * 2 + k
+            arriving.append(pltpu.make_async_copy(src.at[:, rows], halves.at[number], come.at[number]))
+            leaving.append(pltpu.make_async_copy(wholes.at[number], dst.at[0, rows], leave.at[number]))
+    for one in arriving:
+        one.start()
+    grads_in.start()
+    for number in range(4):
+        arriving[number].wait()
+        for k in range(CHIPS):
+            for half in range(2):
+                wholes[number, :, (2 * k + half) * LANE:(2 * k + half + 1) * LANE] = (
+                    halves[number, half, :, k * LANE:(k + 1) * LANE])
+        leaving[number].start()
+    grads_in.wait()
+    grads_away.start()
+    for one in leaving:
+        one.wait()
+    grads_away.wait()
 
 
 def per_device(cotangent, stashed_inputs, weights, momentum):
@@ -521,8 +642,8 @@
         pltpu.VMEM((4, ROWS, 1024), BF),
         pltpu.VMEM((ROWS, HALF), F32),
         pltpu.VMEM((ROWS, HALF), BF),
-        pltpu.VMEM((ROWS, HALF), F32),
-        pltpu.VMEM((ROWS, HALF), BF),
+        pltpu.VMEM((ROWS, WIDTH), BF),
+        pltpu.VMEM((RING, ROWS, HALF), BF),
         pltpu.VMEM((8, LANE), F32),
         pltpu.VMEM((8, LANE), F32),
         pltpu.VMEM((RING, 8, LANE), F32),
@@ -536,8 +657,8 @@
         sem((2, CHIPS)),
         sem((30,)),
         sem((2, CHIPS)),
-        sem((8,)),
-        sem((8,)),
+        sem((10,)),
+        sem((10,)),
         sem((4,)),
         sem((4,)),
         sem((2,)),
@@ -547,21 +668,34 @@
         sem((2, 3)),
         sem((2, RING)),
     ]
+    held = pl.pallas_call(
+        step_kernel,
+        out_shape=(
+            jax.ShapeDtypeStruct(stashed_inputs.shape, BF),
+            jax.ShapeDtypeStruct((2, LANE, HALF), BF),
+            jax.ShapeDtypeStruct((2, LANE, HALF), BF),
+        ),
+        in_specs=[anywhere] * 4,
+        out_specs=(anywhere, anywhere, anywhere),
+        scratch_shapes=scratch,
+        compiler_params=pltpu.CompilerParams(
+            collective_id=0, has_side_effects=True, vmem_limit_bytes=62 * 1024 * 1024),
+        cost_estimate=pl.CostEstimate(
+            flops=22 * 10**9, bytes_accessed=6 * 2**20, transcendentals=32768),
+    )(cotangent, stashed_inputs, weights, momentum)
     return pl.pallas_call(
-        step_kernel,
+        copy_kernel,
         out_shape=(
             jax.ShapeDtypeStruct(stashed_inputs.shape, BF),
             jax.ShapeDtypeStruct(momentum.shape, BF),
             jax.ShapeDtypeStruct(momentum.shape, BF),
         ),
-        in_specs=[anywhere] * 4,
+        in_specs=[anywhere] * 3,
         out_specs=(anywhere, anywhere, anywhere),
-        scratch_shapes=scratch,
-        compiler_params=pltpu.CompilerParams(
-            collective_id=0, has_side_effects=True, vmem_limit_bytes=60 * 1024 * 1024),
-        cost_estimate=pl.CostEstimate(
-            flops=22 * 10**9, bytes_accessed=6 * 2**20, transcendentals=32768),
-    )(cotangent, stashed_inputs, weights, momentum)
+        scratch_shapes=[
+            pltpu.VMEM((1, 2, LANE, LANE), BF), pltpu.VMEM((4, 2, 64, HALF), BF),
+            pltpu.VMEM((4, 64, WIDTH), BF), sem((5,)), sem((5,))],
+    )(*held)
 
 
 def solution(mesh):

time: 146 us -> 140 us (0.959)
  local copies, waits for them, and re-layouts: 4.82 us -> 0 us
    unnamed x5 -> x0, local copies, waits for them, and re-layouts: 4.82 us -> none
    pallas_call x1, Pallas kernels: 140 us -> 137 us  [per_device(): pl.pallas_call(step_kernel, out_shape=(jax.ShapeDtypeStruct(stashed_input...]
    pallas_call x0 -> x1, Pallas kernels: none -> 2.54 us  [per_device(): pl.pallas_call(copy_kernel, out_shape=(jax.ShapeDtypeStruct(stashed_input...]
where the time goes in v3:
time: 140 us
  Pallas kernels  139 us (99%)
    pallas_call x1, Pallas kernels, per_device(): pl.pallas_call(step_kernel, out_shape=(jax.ShapeDtypeStruct(stashed_input...  137 us

profile of v3, /device:TPU:1, one launch (start us, length us, event | category | flops | bytes accessed | tf_op | source)
XLA Modules:
  0.0 140.3 jit_solution(10645179216809865576)
XLA Ops:
  0.6 136.9 %shard_map.67 = (bf16[1,2,128,128]{3,2,1,0:T(8,128)(2,1)}, bf16[2,128,2048]{2,1,0:T(8,128)(2,1)}, bf16[2,128,2048]{2,1,0:T(8,128)(2,1)}) custom-call(bf16[2,128,128]{2,1,0:T(8,128)(2,1)} %cot.1, bf16[1,2,128,128]{3,2,1,0:T(8,128)(2,1)} %xs.1, bf16[1,128,4096]{2,1,0:T(8,128)(2,1)} %w.1, bf16[1,128,4096]{2,1,0:T(8,128)(2,1)} %m.1), custom_call_target="tpu_custom_call" | custom-call | flops 22000001024 | bytes 6291456 | tf_op jit(solution)/shard_map/pallas_call | solution.py:671
  137.6 2.5 %shard_map.68 = (bf16[1,2,128,128]{3,2,1,0:T(8,128)(2,1)}, bf16[1,128,4096]{2,1,0:T(8,128)(2,1)}, bf16[1,128,4096]{2,1,0:T(8,128)(2,1)}) custom-call(bf16[1,2,128,128]{3,2,1,0:T(8,128)(2,1)} %get-tuple-element.6.grads, bf16[2,128,2048]{2,1,0:T(8,128)(2,1)} %get-tuple-element.7.fresh, bf16[2,128,2048]{2,1,0:T(8,128)(2,1)} %get-tuple-element.8.update), custom_call_target="tpu_custom_call" | custom-call | tf_op jit(solution)/shard_map/pallas_call | solution.py:686

commit v4 on v3

--- a/solution.py
+++ b/solution.py
@@ -44,6 +44,10 @@
     return pl.multiple_of(value, of)
 
 
+def offset_of(index):
+    return index + (index // 2) * (5 - 2 * index)
+
+
 def ring(value, steps):
     return (value + steps) % RING
 
@@ -119,8 +123,8 @@
 
 
 DEPTH = 2
-CHUNKS = ((0, 1), (2, 3, 4), (5, 6))
-EXTRA = {3: (0, 1), 2: (2, 3), 1: (5,), 0: (7, 8)}
+CHUNKS = ((0, 1), (2, 3, 4), (5, 6, 7))
+EXTRA = {3: (0, 1), 2: (2, 3), 1: (5,), 0: (8,)}
 
 
 class Bulk:
@@ -197,8 +201,8 @@
 
 def step_kernel(
     cot, xs, w, m, dout, nout, oout,
-    mbuf, nbuf, nrow, wbuf, ubuf, gbuf, xin, slope, dbuf, bsend, brecv, bown, apart, aother, fpart, fother,
-    eacc, ebf, fwhole, stage, own_sum, other_sum, sum_x, sum_z,
+    mbuf, nbuf, nrow, wbuf, ubuf, gbuf, xin, slope, dbuf, bsend, brecv, bown, apart, aother, fother,
+    eacc, ebf, stage, own_sum, other_sum, sum_x, sum_z,
     lsem, sib_send, sib_recv, msend, mrecv, gsend, grecv, usend, urecv,
     asend, arecv, fsend, frecv, osem, orecv, nsem, nrecv, ssend, srecv,
 ):
@@ -363,8 +367,6 @@
         return carry
 
     lax.fori_loop(0, RING, front, 0)
-
-    go(7)
 
     def share(part):
         return remote(gbuf.at[part], gbuf.at[part], sib_send.at[4], sib_recv.at[4])
@@ -421,70 +423,85 @@
             to_ring(buf, axis, steps, ring(own, steps)).wait_recv()
         return buf[0] + buf[1] + buf[2] + buf[3]
 
+    def own_first(part):
+        return x + part * (z - x)
+
+    def own_second(part):
+        return z + part * (x - z)
+
     def group_rows(index, part):
-        first = plane.spot(part, OFFSETS[index], 0)[0]
-        return part, multiple(first * 512, 512)
+        return multiple(ring(own_first(part), offset_of(index)) * 512, 512)
+
+    def both_parts(body):
+        def one(part, carry):
+            body(part)
+            return carry
+
+        lax.fori_loop(0, 2, one, 0)
+
+    def slot_lanes(slot, width):
+        return pl.ds(multiple(slot * width, width), width)
+
+    fpart, fwhole = apart, aother
 
     def a_copy(slot):
-        return remote(apart.at[slot], aother.at[slot], asend.at[slot], arecv.at[slot])
+        lanes = slot_lanes(slot, 512)
+        return remote(apart.at[:, lanes], aother.at[:, lanes], asend.at[slot], arecv.at[slot])
 
     def f_copy(slot):
-        return remote(fpart.at[slot], fother.at[slot], fsend.at[slot], frecv.at[slot])
-
-    def build(index):
-        for part in (0, 1):
-            part, start = group_rows(index, part)
-            rows = pl.ds(part * HALF + start, 512)
+        lanes = slot_lanes(slot, 1024)
+        return remote(fpart.at[:, lanes], fother.at[:, lanes], fsend.at[slot], frecv.at[slot])
+
+    def build_and_gram(index):
+        def body(part):
+            start = group_rows(index, part)
+            rows = pl.ds(multiple(part * HALF + start, 512), 512)
             grad = lax.dot_general(gbuf[part, pl.ds(start, 512), :], ubuf[...], NN,
                                    preferred_element_type=F32)
             nbuf[rows, :] = (0.95 * mbuf[rows, :].astype(F32) + grad).astype(BF)
-
-    def gram(index):
-        for part in (0, 1):
-            part, start = group_rows(index, part)
-            rows = pl.ds(part * HALF + start, 512)
             product = lax.dot_general(nrow[...], nbuf[rows, :], NT, preferred_element_type=F32)
-            apart[index * 2 + part] = (product * inverse).astype(BF)
+            apart[:, slot_lanes(index * 2 + part, 512)] = (product * inverse).astype(BF)
             a_copy(index * 2 + part).start()
 
+        both_parts(body)
+
     def cubic(index):
-        for part in (0, 1):
-            part, start = group_rows(index, part)
-            rows = pl.ds(part * HALF + start, 512)
+        def body(part):
+            rows = pl.ds(multiple(part * HALF + group_rows(index, part), 512), 512)
             slot = index * 2 + part
             a_copy(slot).wait_recv()
-            whole = (apart[slot].astype(F32) + aother[slot].astype(F32)).astype(BF)
-            product = lax.dot_general(whole, nbuf[rows, :], NN, preferred_element_type=F32)
-            if slot == 0:
-                eacc[...] = product
-            else:
-                eacc[...] += product
+            lanes = slot_lanes(slot, 512)
+            whole = (apart[:, lanes].astype(F32) + aother[:, lanes].astype(F32)).astype(BF)
+            eacc[...] += lax.dot_general(whole, nbuf[rows, :], NN, preferred_element_type=F32)
+
+        both_parts(body)
 
     def small(second):
-        parts = []
-        for part in (0, 1):
-            first, last = plane.spot(part, OFFSETS[3], second)
+        def body(part):
+            first, last = ring(own_first(part), OFFSETS[3]), ring(own_second(part), second)
             start = multiple((first * RING + last) * LANE, LANE)
-            rows = pl.ds(part * HALF + start, LANE)
+            rows = pl.ds(multiple(part * HALF + start, LANE), LANE)
             grad = lax.dot_general(gbuf[part, pl.ds(start, LANE), :], ubuf[...], NN,
                                    preferred_element_type=F32)
             fresh = (0.95 * mbuf[rows, :].astype(F32) + grad).astype(BF)
             nbuf[rows, :] = fresh
-            stage[second, pl.ds(part * LANE, LANE), :] = fresh
+            stage[second, pl.ds(multiple(part * LANE, LANE), LANE), :] = fresh
+
+        both_parts(body)
         product = lax.dot_general(nrow[...], stage[second], NT, preferred_element_type=F32)
-        slot, lanes = 6 + second // 2, pl.ds((second % 2) * ROWS, ROWS)
-        apart[slot, :, lanes] = (product * inverse).astype(BF)
+        lanes = slot_lanes(12 + second, ROWS)
+        apart[:, lanes] = (product * inverse).astype(BF)
         small_copy(second).start()
 
     def small_copy(second):
-        slot, lanes = 6 + second // 2, pl.ds((second % 2) * ROWS, ROWS)
-        return remote(apart.at[slot, :, lanes], aother.at[slot, :, lanes],
+        lanes = slot_lanes(12 + second, ROWS)
+        return remote(apart.at[:, lanes], aother.at[:, lanes],
                       asend.at[6 + second], arecv.at[6 + second])
 
     def small_cubic(second):
         small_copy(second).wait_recv()
-        slot, lanes = 6 + second // 2, pl.ds((second % 2) * ROWS, ROWS)
-        whole = (apart[slot, :, lanes].astype(F32) + aother[slot, :, lanes].astype(F32)).astype(BF)
+        lanes = slot_lanes(12 + second, ROWS)
+        whole = (apart[:, lanes].astype(F32) + aother[:, lanes].astype(F32)).astype(BF)
         eacc[...] += lax.dot_general(whole, stage[second], NN, preferred_element_type=F32)
 
     def settle():
@@ -510,77 +527,113 @@
     start_ring(sum_x, 0, x, chip_sum)
     chip_norm = jnp.sqrt(jnp.maximum(jnp.sum(chip_sum), 1e-30))
     inverse = 1.0 / chip_norm
-    bulk.complete(OFFSETS[0])
-    go(9)
-    build(0)
-    gram(0)
-
-    @pl.when(y == 0)
-    def _():
-        back_product()
-
-    go(10)
-    cubic(0)
-    go(11)
-    start_ring(sum_z, 1, z, wait_ring(sum_x, 0, x))
-    bulk.complete(OFFSETS[1])
-    build(1)
-    go(12)
-    gram(1)
-    go(13)
-    cubic(1)
-    small(0)
-    go(14)
-    bulk.wait(2, 1, 0)
-    small(1)
-    small_cubic(0)
-    bulk.wait(2, 3, 1)
-    small(3)
-    small_cubic(1)
-    settle()
-    bulk.complete(OFFSETS[2])
-    build(2)
-    gram(2)
-    small_cubic(3)
+    eacc[...] = jnp.zeros_like(eacc)
+
+    def stream(index, carry):
+        @pl.when(index == 2)
+        def _():
+            def pieces(k, carry):
+                second = offset_of(k)
+
+                @pl.when(k == 1)
+                def _():
+                    bulk.wait(2, 1, 0)
+
+                @pl.when(k == 2)
+                def _():
+                    bulk.wait(2, 3, 1)
+
+                small(second)
+
+                @pl.when(k > 0)
+                def _():
+                    small_cubic(offset_of(k - 1))
+
+                return carry
+
+            lax.fori_loop(0, 3, pieces, 0)
+            settle()
+
+        bulk.complete(offset_of(index))
+
+        @pl.when(index == 0)
+        def _():
+            go(9)
+
+        build_and_gram(index)
+
+        @pl.when(index == 0)
+        def _():
+            @pl.when(y == 0)
+            def _():
+                back_product()
+
+            go(10)
+
+        @pl.when(index == 1)
+        def _():
+            go(12)
+
+        cubic(index)
+
+        @pl.when(index == 0)
+        def _():
+            go(11)
+            start_ring(sum_z, 1, z, wait_ring(sum_x, 0, x))
+
+        @pl.when(index == 1)
+        def _():
+            go(13)
+            go(14)
+
+        return carry
+
+    lax.fori_loop(0, 3, stream, 0)
     sum_squares = jnp.sum(wait_ring(sum_z, 1, z))
     scaling = 0.4 / jnp.sqrt(float(WIDTH) * (sum_squares / float(WIDTH * WIDTH) + 1e-06))
     bulk.wait(2, 2, 0)
     bulk.wait(2, 2, 1)
     small(2)
-    cubic(2)
-    small_cubic(2)
+
+    def last_pieces(k, carry):
+        small_cubic(offset_of(k))
+        return carry
+
+    lax.fori_loop(2, 4, last_pieces, 0)
     ebf[...] = (((eacc[...] * scaling) * scaling) * (scaling * chip_norm)).astype(BF)
 
     for slot in (4, 5):
         a_copy(slot).wait_send()
     small_copy(2).wait_send()
     small_copy(3).wait_send()
-    for steps in (1, 2, 3):
-        to_ring(sum_z, 1, steps, 0).wait_send()
-    for number in range(15 - DEPTH, 15):
-        bulk.sent(number)
-
-    def back_part(slot):
-        product = lax.dot_general(ebf[...], nbuf[pl.ds(slot * 1024, 1024), :], NT, preferred_element_type=F32)
-        fpart[slot] = (product * scaling).astype(BF)
+    obuf = stage.at[0]
+
+    def all_back(slot, carry):
+        product = lax.dot_general(ebf[...], nbuf[pl.ds(multiple(slot * 1024, 1024), 1024), :], NT,
+                                  preferred_element_type=F32)
+        fpart[:, slot_lanes(slot, 1024)] = (product * scaling).astype(BF)
         f_copy(slot).start()
+        return carry
+
+    lax.fori_loop(0, 4, all_back, 0)
 
     def back_whole(slot):
         f_copy(slot).wait_recv()
-        fwhole[:, pl.ds(slot * 1024, 1024)] = (
-            fpart[slot].astype(F32) + fother[slot].astype(F32)).astype(BF)
-
-    obuf = stage.at[0]
-    for slot in range(4):
-        back_part(slot)
+        lanes = slot_lanes(slot, 1024)
+        fwhole[:, lanes] = (fpart[:, lanes].astype(F32) + fother[:, lanes].astype(F32)).astype(BF)
+
     for slot in range(3):
         back_whole(slot)
-    for cut in range(4):
-        lanes = pl.ds(cut * 512, 512)
+
+    def cuts(cut, carry):
+        lanes = pl.ds(multiple(cut * 512, 512), 512)
         product = lax.dot_general(fwhole[:, pl.ds(0, 3072)], nbuf[pl.ds(0, 3072), lanes], NN,
                                   preferred_element_type=F32)
-        if cut == 0:
+
+        @pl.when(cut == 0)
+        def _():
             back_whole(3)
+
         product = product + lax.dot_general(
             fwhole[:, pl.ds(3072, 1024)], nbuf[pl.ds(3072, 1024), lanes], NN, preferred_element_type=F32)
         scaled = (nrow[:, lanes].astype(F32) * scaling).astype(BF).astype(F32)
@@ -588,7 +641,14 @@
                  + quintic_c * (product * scaling))
         obuf[:, lanes] = (math.sqrt(WIDTH) * mixed).astype(BF)
         give_rows(obuf, oout, osem, orecv, lanes)
-
+        return carry
+
+    lax.fori_loop(0, 4, cuts, 0)
+
+    for steps in (1, 2, 3):
+        to_ring(sum_z, 1, steps, 0).wait_send()
+    for number in range(15 - DEPTH, 15):
+        bulk.sent(number)
     for slot in range(4):
         f_copy(slot).wait_send()
     wait_rows(obuf, osem, orecv)
@@ -636,13 +696,11 @@
         pltpu.VMEM((TOKENS, LANE), F32),
         pltpu.VMEM((TOKENS, LANE), F32),
         pltpu.VMEM((TOKENS, LANE), F32),
-        pltpu.VMEM((8, ROWS, 512), BF),
-        pltpu.VMEM((8, ROWS, 512), BF),
-        pltpu.VMEM((4, ROWS, 1024), BF),
-        pltpu.VMEM((4, ROWS, 1024), BF),
+        pltpu.VMEM((ROWS, WIDTH), BF),
+        pltpu.VMEM((ROWS, WIDTH), BF),
+        pltpu.VMEM((ROWS, WIDTH), BF),
         pltpu.VMEM((ROWS, HALF), F32),
         pltpu.VMEM((ROWS, HALF), BF),
-        pltpu.VMEM((ROWS, WIDTH), BF),
         pltpu.VMEM((RING, ROWS, HALF), BF),
         pltpu.VMEM((8, LANE), F32),
         pltpu.VMEM((8, LANE), F32),

time: 140 us -> 135 us (0.964)
  Pallas kernels: 139 us -> 134 us
    pallas_call x1, Pallas kernels: 137 us -> 132 us  [per_device(): pl.pallas_call(step_kernel, out_shape=(jax.ShapeDtypeStruct(stashed_input...]
where the time goes in v4:
time: 135 us
  Pallas kernels  134 us (99%)
    pallas_call x1, Pallas kernels, per_device(): pl.pallas_call(step_kernel, out_shape=(jax.ShapeDtypeStruct(stashed_input...  132 us

profile of v4, /device:TPU:1, one launch (start us, length us, event | category | flops | bytes accessed | tf_op | source)
XLA Modules:
  0.0 134.9 jit_solution(514310918939140715)
XLA Ops:
  0.6 131.7 %shard_map.67 = (bf16[1,2,128,128]{3,2,1,0:T(8,128)(2,1)}, bf16[2,128,2048]{2,1,0:T(8,128)(2,1)}, bf16[2,128,2048]{2,1,0:T(8,128)(2,1)}) custom-call(bf16[2,128,128]{2,1,0:T(8,128)(2,1)} %cot.1, bf16[1,2,128,128]{3,2,1,0:T(8,128)(2,1)} %xs.1, bf16[1,128,4096]{2,1,0:T(8,128)(2,1)} %w.1, bf16[1,128,4096]{2,1,0:T(8,128)(2,1)} %m.1), custom_call_target="tpu_custom_call" | custom-call | flops 22000001024 | bytes 6291456 | tf_op jit(solution)/shard_map/pallas_call | solution.py:729
  132.3 2.5 %shard_map.68 = (bf16[1,2,128,128]{3,2,1,0:T(8,128)(2,1)}, bf16[1,128,4096]{2,1,0:T(8,128)(2,1)}, bf16[1,128,4096]{2,1,0:T(8,128)(2,1)}) custom-call(bf16[1,2,128,128]{3,2,1,0:T(8,128)(2,1)} %get-tuple-element.6.grads, bf16[2,128,2048]{2,1,0:T(8,128)(2,1)} %get-tuple-element.7.fresh, bf16[2,128,2048]{2,1,0:T(8,128)(2,1)} %get-tuple-element.8.update), custom_call_target="tpu_custom_call" | custom-call | tf_op jit(solution)/shard_map/pallas_call | solution.py:744

commit v5 on v4

--- a/solution.py
+++ b/solution.py
@@ -124,7 +124,7 @@
 
 DEPTH = 2
 CHUNKS = ((0, 1), (2, 3, 4), (5, 6, 7))
-EXTRA = {3: (0, 1), 2: (2, 3), 1: (5,), 0: (8,)}
+EXTRA = {3: (0, 1), 2: (2, 3), 1: (5,), 0: (8, 9)}
 
 
 class Bulk:

time: 135 us -> 134 us (level)
  no operation moved by 1% of the time
where the time goes in v5:
time: 134 us
  Pallas kernels  133 us (99%)
    pallas_call x1, Pallas kernels, per_device(): pl.pallas_call(step_kernel, out_shape=(jax.ShapeDtypeStruct(stashed_input...  131 us

profile of v5, /device:TPU:1, one launch (start us, length us, event | category | flops | bytes accessed | tf_op | source)
XLA Modules:
  0.0 133.8 jit_solution(16807989082769314568)
XLA Ops:
  0.6 130.6 %shard_map.67 = (bf16[1,2,128,128]{3,2,1,0:T(8,128)(2,1)}, bf16[2,128,2048]{2,1,0:T(8,128)(2,1)}, bf16[2,128,2048]{2,1,0:T(8,128)(2,1)}) custom-call(bf16[2,128,128]{2,1,0:T(8,128)(2,1)} %cot.1, bf16[1,2,128,128]{3,2,1,0:T(8,128)(2,1)} %xs.1, bf16[1,128,4096]{2,1,0:T(8,128)(2,1)} %w.1, bf16[1,128,4096]{2,1,0:T(8,128)(2,1)} %m.1), custom_call_target="tpu_custom_call" | custom-call | flops 22000001024 | bytes 6291456 | tf_op jit(solution)/shard_map/pallas_call | solution.py:729
  131.2 2.5 %shard_map.68 = (bf16[1,2,128,128]{3,2,1,0:T(8,128)(2,1)}, bf16[1,128,4096]{2,1,0:T(8,128)(2,1)}, bf16[1,128,4096]{2,1,0:T(8,128)(2,1)}) custom-call(bf16[1,2,128,128]{3,2,1,0:T(8,128)(2,1)} %get-tuple-element.6.grads, bf16[2,128,2048]{2,1,0:T(8,128)(2,1)} %get-tuple-element.7.fresh, bf16[2,128,2048]{2,1,0:T(8,128)(2,1)} %get-tuple-element.8.update), custom_call_target="tpu_custom_call" | custom-call | tf_op jit(solution)/shard_map/pallas_call | solution.py:744
